TPU v7x, 32 devices: a whole 2x2x4 slice. The times are simulated.
32 devices in a mesh: head: 8 (over z, x), blk: 4 (over y, core).
Axes of the slice: x: 2, y: 2, z: 4, core: 2. Of those that a mesh axis runs over, the one named last changes fastest.
Arguments:
- tokens: bfloat16 [8192, 1024], P(('blk', 'head')), may hold values from -6 to 6
- w_proj: bfloat16 [1024, 4096], replicated, may hold values from -0.1875 to 0.1875
- w_out: bfloat16 [1024, 1024], replicated, may hold values from -0.1875 to 0.1875
- cotangent: bfloat16 [8192, 1024], P(('blk', 'head')), may hold values from -6 to 6
- key_blocks: int32 [64, 8], P('blk'), may hold values from 0 to 63, as said below
- exposures: int32 [64, 8], P('blk'), may hold values from 0 to 16, as said below
- positions: int32 [8192], replicated, may hold values from 0 to 4096, as said below
Outputs:
- mixed: bfloat16 [8192, 1024], P(('blk', 'head'))
- grad_u: bfloat16 [1024, 8192], P(None, ('blk', 'head'))
- grad_qkv: float32 [3, 1024, 8192], P(None, 'head', 'blk')
Inputs may be any that keep to these rules, and one draw needn't show every extreme that they name: `key_blocks`: every entry is at most its row's index; the first entry of each row is the row's own index; the entries of a row with a nonzero exposure are distinct. `exposures`: the first slot of every row is at least 1; a slot is 0 only in rows with fewer than 8 earlier blocks. `positions`: nondecreasing along the history, starting at 0, rising by 0 or 1 from one event to the next.
All inputs are finite; a program needn't handle non-finite values.
Results may differ from a plain program's by a relative error of at most 0.0083.
Values may be sent and summed in bfloat16 or wider, within the bound.
A program may use at most 128 MiB of HBM per device.

v0:
```python
import math

import jax
import jax.numpy as jnp
from jax import lax
from jax.sharding import PartitionSpec as P

HEADS = 32
HEAD_DIM = 32
BLOCK = 128


epsilon = 1e-05


def silu_slope(values):
    sigmoid = jax.nn.sigmoid(values)
    return sigmoid * (1.0 + values * (1.0 - sigmoid))


def shards(tokens, w_proj, w_out, cotangent, key_blocks, exposures, positions):
    head_count = lax.axis_size("head")
    group_count = lax.axis_size("blk")
    segment_index = lax.axis_index("blk")
    local_rows, width = tokens.shape
    heads_here = HEADS // head_count
    segment = local_rows * head_count
    total_rows = segment * group_count
    all_blocks = total_rows // BLOCK
    local_blocks = segment // BLOCK
    per_step = math.gcd(local_blocks, max(1, 512 // BLOCK))
    steps_count = local_blocks // per_step
    scaling = HEAD_DIM ** (-0.5)
    projected = jax.nn.silu(
        lax.dot_general(
            w_proj, tokens, (((0,), (1,)), ((), ())), preferred_element_type=jnp.float32
        )
    ).astype(jnp.bfloat16)
    projected = projected.reshape(4, HEADS, HEAD_DIM, local_rows)
    gate_u = projected[0].reshape(width, local_rows).astype(jnp.float32)
    by_head = lax.all_to_all(projected[1:], "head", split_axis=1, concat_axis=3, tiled=True)
    query = by_head[0].reshape(heads_here, HEAD_DIM, local_blocks, BLOCK)
    key_vals = by_head[1:]
    key_all = lax.all_gather(key_vals, "blk", axis=3, tiled=True)
    key_all = key_all.reshape(2, heads_here, HEAD_DIM, all_blocks, BLOCK)
    key_table = jnp.transpose(key_all[0], (2, 0, 1, 3))
    value_table = jnp.transpose(key_all[1], (2, 0, 1, 3))
    pos_blocks = positions.reshape(all_blocks, BLOCK)
    query_positions = lax.dynamic_slice_in_dim(
        pos_blocks, segment_index * local_blocks, local_blocks, 0
    )
    weights = jnp.log1p(exposures.astype(jnp.float32))

    def gather_group(start):
        chosen = lax.dynamic_slice_in_dim(key_blocks, start, per_step, 0)
        query_group = lax.dynamic_slice_in_dim(query, start, per_step, 2)
        key_group = jnp.take(key_table, chosen, axis=0)
        value_group = jnp.take(value_table, chosen, axis=0)
        weights_group = lax.dynamic_slice_in_dim(weights, start, per_step, 0)
        query_pos = lax.dynamic_slice_in_dim(query_positions, start, per_step, 0)
        key_pos = jnp.take(pos_blocks, chosen, axis=0)
        scores = (
            jnp.einsum(
                "hegb,gkhec->hgbkc", query_group, key_group, preferred_element_type=jnp.float32
            )
            * scaling
        )
        allowed = key_pos[:, None, :, :] <= query_pos[:, :, None, None]
        coefficient = jnp.where(allowed, weights_group[:, None, :, None], 0.0)
        weighted = (jax.nn.silu(scores) * coefficient).astype(jnp.bfloat16)
        return (chosen, query_group, key_group, value_group, scores, coefficient, weighted)

    def forward_step(number, attended):
        start = number * per_step
        terms = gather_group(start)
        result = jnp.einsum(
            "hgbkc,gkhec->hegb", terms[6], terms[3], preferred_element_type=jnp.float32
        )
        return lax.dynamic_update_slice_in_dim(attended, result.astype(jnp.bfloat16), start, 2)

    attended = lax.fori_loop(
        0,
        steps_count,
        forward_step,
        jnp.zeros((heads_here, HEAD_DIM, local_blocks, BLOCK), jnp.bfloat16),
    )
    attended = attended.reshape(heads_here, HEAD_DIM, segment)
    by_token = (
        lax.all_to_all(attended, "head", split_axis=2, concat_axis=0, tiled=True)
        .reshape(width, local_rows)
        .astype(jnp.float32)
    )
    average = jnp.mean(by_token, axis=0)
    centered = by_token - average
    variance = jnp.mean(centered * centered, axis=0)
    inverse_std = lax.rsqrt(variance + epsilon)
    normed = centered * inverse_std
    gated = (normed * gate_u).astype(jnp.bfloat16)
    mixed = (
        tokens.astype(jnp.float32)
        + lax.dot_general(
            gated, w_out, (((0,), (0,)), ((), ())), preferred_element_type=jnp.float32
        )
    ).astype(jnp.bfloat16)
    d_gated = lax.dot_general(
        w_out, cotangent, (((1,), (1,)), ((), ())), preferred_element_type=jnp.float32
    )
    grad_u = (d_gated * normed).astype(jnp.bfloat16)
    d_normed = d_gated * gate_u
    d_attended = inverse_std * (
        d_normed - jnp.mean(d_normed, axis=0) - normed * jnp.mean(d_normed * normed, axis=0)
    )
    d_attended = d_attended.astype(jnp.bfloat16).reshape(HEADS, HEAD_DIM, local_rows)
    d_heads = lax.all_to_all(d_attended, "head", split_axis=0, concat_axis=2, tiled=True).reshape(
        heads_here, HEAD_DIM, local_blocks, BLOCK
    )

    def backward_step(number, carry):
        grad_query, grad_keys, grad_values = carry
        start = number * per_step
        chosen, query_group, key_group, value_group, scores, coefficient, weighted = gather_group(
            start
        )
        d_group = lax.dynamic_slice_in_dim(d_heads, start, per_step, 2)
        d_values = jnp.einsum(
            "hgbkc,hegb->gkhec", weighted, d_group, preferred_element_type=jnp.float32
        )
        d_weighted = jnp.einsum(
            "hegb,gkhec->hgbkc", d_group, value_group, preferred_element_type=jnp.float32
        )
        d_scores = (d_weighted * coefficient * silu_slope(scores)).astype(jnp.bfloat16)
        d_query = (
            jnp.einsum("hgbkc,gkhec->hegb", d_scores, key_group, preferred_element_type=jnp.float32)
            * scaling
        )
        d_keys = (
            jnp.einsum(
                "hgbkc,hegb->gkhec", d_scores, query_group, preferred_element_type=jnp.float32
            )
            * scaling
        )
        grad_query = lax.dynamic_update_slice_in_dim(grad_query, d_query, start, 2)
        grad_keys = grad_keys.at[chosen].add(d_keys)
        grad_values = grad_values.at[chosen].add(d_values)
        return (grad_query, grad_keys, grad_values)

    start_query = jnp.zeros((heads_here, HEAD_DIM, local_blocks, BLOCK), jnp.float32)
    start_table = jnp.zeros((all_blocks, heads_here, HEAD_DIM, BLOCK), jnp.float32)
    grad_query, grad_keys, grad_values = lax.fori_loop(
        0, steps_count, backward_step, (start_query, start_table, start_table)
    )
    key_partial = jnp.transpose(jnp.stack([grad_keys, grad_values]), (0, 2, 3, 1, 4)).reshape(
        2, heads_here, HEAD_DIM, total_rows
    )
    summed = lax.psum_scatter(
        key_partial.astype(jnp.bfloat16), "blk", scatter_dimension=3, tiled=True
    ).astype(jnp.float32)
    grad_qkv = jnp.concatenate(
        [
            grad_query.reshape(1, heads_here * HEAD_DIM, segment),
            summed.reshape(2, heads_here * HEAD_DIM, segment),
        ],
        axis=0,
    )
    return (mixed, grad_u, grad_qkv)


def solution(mesh):
    in_specs = (
        P(("blk", "head"), None),
        P(),
        P(),
        P(("blk", "head"), None),
        P("blk", None),
        P("blk", None),
        P(),
    )
    out_specs = (P(("blk", "head"), None), P(None, ("blk", "head")), P(None, "head", "blk"))
    return jax.shard_map(shards, mesh=mesh, in_specs=in_specs, out_specs=out_specs, check_vma=False)
```

profile of v0, /device:TPU:11, one launch (start us, length us, event | category | flops | bytes accessed | tf_op | source)
XLA Modules:
  0.0 461.7 jit_solution(11921937271932613061)
XLA Ops:
  7.2 6.6 %multiply_convert_fusion.12 = bf16[4096,256]{1,0:T(8,128)(2,1)S(1)} fusion(bf16[1024,4096]{1,0:T(8,128)(2,1)} %param.16, bf16[256,1024]{1,0:T(8,128)(2,1)} %param.15), kind=kOutput, calls=%fused_computation.74 | convolution fusion | flops 2152726528 | bytes 11010048 | tf_op jit(solution)/shard_map/dot_general | solution.py:35
  14.0 39.6 %all_to_all.39 = bf16[3,32,32,256]{3,2,0,1:T(8,128)(2,1)S(1)} all-to-all(bf16[3,32,32,256]{3,2,0,1:T(8,128)(2,1)S(1)} %copy.114), channel_id=1, replica_groups=mesh['head'=8,'blk'=4] {'head'}, dimensions={1} | all-to-all | bytes 3145728 | tf_op jit(solution)/shard_map/all_to_all | solution.py:41
  58.9 34.5 %all-gather.2.cloned.1.call-done = bf16[2,4,32,8192]{3,2,1,0:T(8,128)(2,1)} async-done(((bf16[2,4,32,2048]{3,2,1,0:T(8,128)(2,1)}), bf16[2,4,32,8192]{3,2,1,0:T(8,128)(2,1)}) %all-gather.2.cloned.1.call-update) | async-done | bytes 4194320 | tf_op jit(solution)/shard_map/all_gather | solution.py:44
  103.9 60.6 %while.30 = (s32[]{:T(128)}, bf16[4,32,16,128]{3,1,2,0:T(8,128)(2,1)}, s32[16,8]{1,0:T(8,128)S(1)}, bf16[64,4,32,128]{3,2,1,0:T(8,128)(2,1)}, bf16[4,32,16,128]{...) while((s32[]{:T(128)}, ...), condition=%wide.region_1.4_spmd, body=%wide.region_0.3_spmd.sunk | while | flops 285283520 | bytes 10843767 | solution.py:81
  111.9 7.1 %fusion.70 = bf16[4,32,16,128]{3,1,2,0:T(8,128)(2,1)} fusion(bf16[4,32,16,128]{3,1,2,0:T(8,128)(2,1)} %get-tuple-element.681, s32[]{:T(128)S(6)} %select_n.126, f32[4,128,8,128]{3,1,2,0:T(8,128)} %compare_select_fusion.8, bf16[4,8,4,32,128]{4,3,2,1,0:T(8,128)(2,1)} %bitcast.189, bf16[4,8,4,32,128]{4,3,2,1,0:T(8,128)(2,1)S(1)} %bitcast.188, ...), kind=kOutput, calls=%fused_computation.15.clone.1 | convolution fusion | flops 284229632 | bytes 4458496 | tf_op jit(solution)/shard_map/while/body/eval_jaxpr/hgbkc,gkhec->hegb/dot_general | solution.py:76
  127.1 7.1 %fusion.70 = bf16[4,32,16,128]{3,1,2,0:T(8,128)(2,1)} fusion(bf16[4,32,16,128]{3,1,2,0:T(8,128)(2,1)} %get-tuple-element.681, s32[]{:T(128)S(6)} %select_n.126, f32[4,128,8,128]{3,1,2,0:T(8,128)} %compare_select_fusion.8, bf16[4,8,4,32,128]{4,3,2,1,0:T(8,128)(2,1)} %bitcast.189, bf16[4,8,4,32,128]{4,3,2,1,0:T(8,128)(2,1)S(1)} %bitcast.188, ...), kind=kOutput, calls=%fused_computation.15.clone.1 | convolution fusion | flops 284229632 | bytes 4458496 | tf_op jit(solution)/shard_map/while/body/eval_jaxpr/hgbkc,gkhec->hegb/dot_general | solution.py:76
  142.2 7.1 %fusion.70 = bf16[4,32,16,128]{3,1,2,0:T(8,128)(2,1)} fusion(bf16[4,32,16,128]{3,1,2,0:T(8,128)(2,1)} %get-tuple-element.681, s32[]{:T(128)S(6)} %select_n.126, f32[4,128,8,128]{3,1,2,0:T(8,128)} %compare_select_fusion.8, bf16[4,8,4,32,128]{4,3,2,1,0:T(8,128)(2,1)} %bitcast.189, bf16[4,8,4,32,128]{4,3,2,1,0:T(8,128)(2,1)S(1)} %bitcast.188, ...), kind=kOutput, calls=%fused_computation.15.clone.1 | convolution fusion | flops 284229632 | bytes 4458496 | tf_op jit(solution)/shard_map/while/body/eval_jaxpr/hgbkc,gkhec->hegb/dot_general | solution.py:76
  157.4 7.1 %fusion.70 = bf16[4,32,16,128]{3,1,2,0:T(8,128)(2,1)} fusion(bf16[4,32,16,128]{3,1,2,0:T(8,128)(2,1)} %get-tuple-element.681, s32[]{:T(128)S(6)} %select_n.126, f32[4,128,8,128]{3,1,2,0:T(8,128)} %compare_select_fusion.8, bf16[4,8,4,32,128]{4,3,2,1,0:T(8,128)(2,1)} %bitcast.189, bf16[4,8,4,32,128]{4,3,2,1,0:T(8,128)(2,1)S(1)} %bitcast.188, ...), kind=kOutput, calls=%fused_computation.15.clone.1 | convolution fusion | flops 284229632 | bytes 4458496 | tf_op jit(solution)/shard_map/while/body/eval_jaxpr/hgbkc,gkhec->hegb/dot_general | solution.py:76
  168.5 4.8 %reshape.211 = bf16[8,2,16384]{2,1,0:T(2,128)(2,1)} reshape(bf16[2048,4,32]{2,1,0:T(4,128)(2,1)} %bitcast.190) | data formatting | bytes 1048576
  173.3 5.5 %all-to-all-start.1 = ((bf16[8,2,16384]{2,1,0:T(2,128)(2,1)}), bf16[8,2,16384]{2,1,0:T(2,128)(2,1)S(1)}, u32[]{:S(2)}, u32[]{:S(2)}) async-start(bf16[8,2,16384]{2,1,0:T(2,128)(2,1)} %reshape.211), calls=%async_computation.1 | async-start | bytes 1048576 | tf_op jit(solution)/shard_map/all_to_all | solution.py:89
  178.8 12.0 %all-to-all-done.1 = bf16[8,2,16384]{2,1,0:T(2,128)(2,1)S(1)} async-done(((bf16[8,2,16384]{2,1,0:T(2,128)(2,1)}), bf16[8,2,16384]{2,1,0:T(2,128)(2,1)S(1)}, u32[]{:S(2)}, u32[]{:S(2)}) %all-to-all-start.1) | async-done | bytes 524320 | tf_op jit(solution)/shard_map/all_to_all | solution.py:89
  192.8 16.5 %convert_reduce_fusion = f32[2048]{0:T(1024)S(1)} fusion(bf16[2048,4,32]{2,1,0:T(4,128)(2,1)} %reshape.212), kind=kLoop, calls=%fused_computation.89 | loop fusion | flops 522240 | bytes 532480 | tf_op jit(solution)/shard_map/reduce_sum | solution.py:93
  221.9 6.3 %all-to-all-start.2 = ((bf16[32,32,256]{2,1,0:T(8,128)(2,1)}), bf16[32,32,256]{2,1,0:T(8,128)(2,1)S(1)}, u32[]{:S(2)}, u32[]{:S(2)}) async-start(bf16[32,32,256]{2,1,0:T(8,128)(2,1)} %bitcast.199), calls=%async_computation.2 | async-start | bytes 1048576 | tf_op jit(solution)/shard_map/all_to_all | solution.py:114
  228.2 12.0 %all-to-all-done.2 = bf16[32,32,256]{2,1,0:T(8,128)(2,1)S(1)} async-done(((bf16[32,32,256]{2,1,0:T(8,128)(2,1)}), bf16[32,32,256]{2,1,0:T(8,128)(2,1)S(1)}, u32[]{:S(2)}, u32[]{:S(2)}) %all-to-all-start.2) | async-done | bytes 524320 | tf_op jit(solution)/shard_map/all_to_all | solution.py:114
  246.7 151.4 %while.31 = (s32[]{:T(128)}, f32[4,32,16,128]{3,2,1,0:T(8,128)}, f32[64,4,32,128]{3,2,1,0:T(8,128)}, f32[64,4,32,128]{3,2,1,0:T(8,128)}, s32[16,8]{1,0:T(8,128)S...) while((s32[]{:T(128)}, f32[4,32,16,128]{3,2,1,0:T(8,128)}, ...), condition=%wide.region_10.13_spmd, body=%wide.region_7.12_spmd.sunk | while | flops 713102528 | bytes 86601808 | solution.py:149
  270.6 7.1 %scatter_fusion.1 = f32[64,4,32,128]{3,2,1,0:T(8,128)} fusion(f32[64,4,32,128]{3,2,1,0:T(8,128)} %get-tuple-element.725, s32[32]{0:T(128)S(1)} %reshape.248, f32[32,4,32,128]{3,2,1,0:T(8,128)} %bitcast.180), kind=kCustom, calls=%fused_computation.7.clone.1 | custom fusion | flops 524288 | bytes 6291584 | tf_op jit(solution)/shard_map/while/body/eval_jaxpr/scatter-add | solution.py:144
  277.6 7.1 %scatter_fusion = f32[64,4,32,128]{3,2,1,0:T(8,128)} fusion(f32[64,4,32,128]{3,2,1,0:T(8,128)} %get-tuple-element.724, s32[32]{0:T(128)S(1)} %reshape.248, f32[32,4,32,128]{3,2,1,0:T(8,128)} %bitcast.179), kind=kCustom, calls=%fused_computation.6.clone.1 | custom fusion | flops 524288 | bytes 6291584 | tf_op jit(solution)/shard_map/while/body/eval_jaxpr/scatter-add | solution.py:143
  308.3 7.0 %scatter_fusion.1 = f32[64,4,32,128]{3,2,1,0:T(8,128)} fusion(f32[64,4,32,128]{3,2,1,0:T(8,128)} %get-tuple-element.725, s32[32]{0:T(128)S(1)} %reshape.248, f32[32,4,32,128]{3,2,1,0:T(8,128)} %bitcast.180), kind=kCustom, calls=%fused_computation.7.clone.1 | custom fusion | flops 524288 | bytes 6291584 | tf_op jit(solution)/shard_map/while/body/eval_jaxpr/scatter-add | solution.py:144
  315.3 7.1 %scatter_fusion = f32[64,4,32,128]{3,2,1,0:T(8,128)} fusion(f32[64,4,32,128]{3,2,1,0:T(8,128)} %get-tuple-element.724, s32[32]{0:T(128)S(1)} %reshape.248, f32[32,4,32,128]{3,2,1,0:T(8,128)} %bitcast.179), kind=kCustom, calls=%fused_computation.6.clone.1 | custom fusion | flops 524288 | bytes 6291584 | tf_op jit(solution)/shard_map/while/body/eval_jaxpr/scatter-add | solution.py:143
  346.0 7.0 %scatter_fusion.1 = f32[64,4,32,128]{3,2,1,0:T(8,128)} fusion(f32[64,4,32,128]{3,2,1,0:T(8,128)} %get-tuple-element.725, s32[32]{0:T(128)S(1)} %reshape.248, f32[32,4,32,128]{3,2,1,0:T(8,128)} %bitcast.180), kind=kCustom, calls=%fused_computation.7.clone.1 | custom fusion | flops 524288 | bytes 6291584 | tf_op jit(solution)/shard_map/while/body/eval_jaxpr/scatter-add | solution.py:144
  353.1 7.1 %scatter_fusion = f32[64,4,32,128]{3,2,1,0:T(8,128)} fusion(f32[64,4,32,128]{3,2,1,0:T(8,128)} %get-tuple-element.724, s32[32]{0:T(128)S(1)} %reshape.248, f32[32,4,32,128]{3,2,1,0:T(8,128)} %bitcast.179), kind=kCustom, calls=%fused_computation.6.clone.1 | custom fusion | flops 524288 | bytes 6291584 | tf_op jit(solution)/shard_map/while/body/eval_jaxpr/scatter-add | solution.py:143
  383.8 7.2 %scatter_fusion.1 = f32[64,4,32,128]{3,2,1,0:T(8,128)} fusion(f32[64,4,32,128]{3,2,1,0:T(8,128)} %get-tuple-element.725, s32[32]{0:T(128)S(1)} %reshape.248, f32[32,4,32,128]{3,2,1,0:T(8,128)} %bitcast.180), kind=kCustom, calls=%fused_computation.7.clone.1 | custom fusion | flops 524288 | bytes 6291584 | tf_op jit(solution)/shard_map/while/body/eval_jaxpr/scatter-add | solution.py:144
  391.0 7.1 %scatter_fusion = f32[64,4,32,128]{3,2,1,0:T(8,128)} fusion(f32[64,4,32,128]{3,2,1,0:T(8,128)} %get-tuple-element.724, s32[32]{0:T(128)S(1)} %reshape.248, f32[32,4,32,128]{3,2,1,0:T(8,128)} %bitcast.179), kind=kCustom, calls=%fused_computation.6.clone.1 | custom fusion | flops 524288 | bytes 6291584 | tf_op jit(solution)/shard_map/while/body/eval_jaxpr/scatter-add | solution.py:143
  408.4 41.3 %reduce-scatter.2.cloned.1.call-done = bf16[2,4,32,2048]{3,2,1,0:T(8,128)(2,1)} async-done(((bf16[2,4,32,8192]{3,2,1,0:T(8,128)(2,1)}), bf16[2,4,32,2048]{3,2,1,0:T(8,128)(2,1)}) %reduce-scatter.2.cloned.1.call-update) | async-done | bytes 1048592 | tf_op jit(solution)/shard_map/reduce_scatter | solution.py:155
  (205 shorter events, 182.4 us)
Async XLA Ops:
  7.2 210.0 %copy-start = (bf16[1024,1024]{1,0:T(8,128)(2,1)S(1)}, bf16[1024,1024]{1,0:T(8,128)(2,1)}, u32[]{:S(2)}) copy-start(bf16[1024,1024]{1,0:T(8,128)(2,1)} %param.17) | copy-start | bytes 6291460
  7.2 86.2 %all-gather.2.cloned.1.call-start = ((), (), s32[]{:S(2)}) async-start(), calls=%async_computation.4 | async-start | bytes 5242880 | tf_op jit(solution)/shard_map/all_gather | solution.py:44
  13.8 39.9 %copy-start.8 = (bf16[4096,256]{1,0:T(8,128)(2,1)}, bf16[4096,256]{1,0:T(8,128)(2,1)S(1)}, u32[]{:S(2)}) copy-start(bf16[4096,256]{1,0:T(8,128)(2,1)S(1)} %multiply_convert_fusion.12) | copy-start | bytes 6291460
  53.6 2.6 copy-start.9
  53.6 2.6 copy-start.10
  53.6 2.7 copy-start.2
  53.8 1.1 copy-start.4
  173.3 17.4 %all-to-all-start.1 = ((bf16[8,2,16384]{2,1,0:T(2,128)(2,1)}), bf16[8,2,16384]{2,1,0:T(2,128)(2,1)S(1)}, u32[]{:S(2)}, u32[]{:S(2)}) async-start(bf16[8,2,16384]{2,1,0:T(2,128)(2,1)} %reshape.211), calls=%async_computation.1 | async-start | bytes 1048576 | tf_op jit(solution)/shard_map/all_to_all | solution.py:89
  221.9 18.3 %all-to-all-start.2 = ((bf16[32,32,256]{2,1,0:T(8,128)(2,1)}), bf16[32,32,256]{2,1,0:T(8,128)(2,1)S(1)}, u32[]{:S(2)}, u32[]{:S(2)}) async-start(bf16[32,32,256]{2,1,0:T(8,128)(2,1)} %bitcast.199), calls=%async_computation.2 | async-start | bytes 1048576 | tf_op jit(solution)/shard_map/all_to_all | solution.py:114
  228.2 221.5 %reduce-scatter.2.cloned.1.call-start = ((), (), s32[]{:S(2)}) async-start(), calls=%async_computation.5 | async-start | bytes 5242880 | tf_op jit(solution)/shard_map/reduce_scatter | solution.py:155
  247.0 4.1 copy-start.6
  253.8 4.7 %copy-start.3 = (bf16[32,4,32,128]{3,2,1,0:T(8,128)(2,1)S(1)}, bf16[32,4,32,128]{3,2,1,0:T(8,128)(2,1)}, u32[]{:S(2)}) copy-start(bf16[32,4,32,128]{3,2,1,0:T(8,128)(2,1)} %gather_fusion.5) | copy-start | bytes 3145732 | tf_op jit(solution)/shard_map/while
  277.6 7.1 %copy-start.7 = (bf16[4,32,16,128]{3,2,1,0:T(8,128)(2,1)S(1)}, bf16[4,32,16,128]{3,2,1,0:T(8,128)(2,1)}, u32[]{:S(2)}) copy-start(bf16[4,32,16,128]{3,2,1,0:T(8,128)(2,1)} %copy-done.6) | copy-start | bytes 1572868 | tf_op jit(solution)/shard_map/while
  284.7 4.1 copy-start.6
  291.5 4.7 %copy-start.3 = (bf16[32,4,32,128]{3,2,1,0:T(8,128)(2,1)S(1)}, bf16[32,4,32,128]{3,2,1,0:T(8,128)(2,1)}, u32[]{:S(2)}) copy-start(bf16[32,4,32,128]{3,2,1,0:T(8,128)(2,1)} %gather_fusion.5) | copy-start | bytes 3145732 | tf_op jit(solution)/shard_map/while
  315.3 7.1 %copy-start.7 = (bf16[4,32,16,128]{3,2,1,0:T(8,128)(2,1)S(1)}, bf16[4,32,16,128]{3,2,1,0:T(8,128)(2,1)}, u32[]{:S(2)}) copy-start(bf16[4,32,16,128]{3,2,1,0:T(8,128)(2,1)} %copy-done.6) | copy-start | bytes 1572868 | tf_op jit(solution)/shard_map/while
  322.4 4.1 copy-start.6
  329.2 4.7 %copy-start.3 = (bf16[32,4,32,128]{3,2,1,0:T(8,128)(2,1)S(1)}, bf16[32,4,32,128]{3,2,1,0:T(8,128)(2,1)}, u32[]{:S(2)}) copy-start(bf16[32,4,32,128]{3,2,1,0:T(8,128)(2,1)} %gather_fusion.5) | copy-start | bytes 3145732 | tf_op jit(solution)/shard_map/while
  353.1 7.1 %copy-start.7 = (bf16[4,32,16,128]{3,2,1,0:T(8,128)(2,1)S(1)}, bf16[4,32,16,128]{3,2,1,0:T(8,128)(2,1)}, u32[]{:S(2)}) copy-start(bf16[4,32,16,128]{3,2,1,0:T(8,128)(2,1)} %copy-done.6) | copy-start | bytes 1572868 | tf_op jit(solution)/shard_map/while
  360.1 4.1 copy-start.6
  367.0 4.7 %copy-start.3 = (bf16[32,4,32,128]{3,2,1,0:T(8,128)(2,1)S(1)}, bf16[32,4,32,128]{3,2,1,0:T(8,128)(2,1)}, u32[]{:S(2)}) copy-start(bf16[32,4,32,128]{3,2,1,0:T(8,128)(2,1)} %gather_fusion.5) | copy-start | bytes 3145732 | tf_op jit(solution)/shard_map/while
  391.0 7.2 %copy-start.7 = (bf16[4,32,16,128]{3,2,1,0:T(8,128)(2,1)S(1)}, bf16[4,32,16,128]{3,2,1,0:T(8,128)(2,1)}, u32[]{:S(2)}) copy-start(bf16[4,32,16,128]{3,2,1,0:T(8,128)(2,1)} %copy-done.6) | copy-start | bytes 1572868 | tf_op jit(solution)/shard_map/while
  398.1 3.4 copy-start.1
  404.4 2.8 copy-start.5
Sparse Core Ops, SparseCore 0:
  56.3 36.9 all-gather.1
  404.5 45.1 reduce-scatter.1
where the time goes:
time: 468 us; the launch traced here: 462 us
  local copies, waits for them, and re-layouts  108 us (23%)
  waiting for transfers between devices  99.7 us (21%)
  other arithmetic  96.8 us (21%)
  matrix products  90.6 us (19%)
  blocking collectives  39.6 us (8%)
  between operations  14.7 us (3%)
  starting transfers between devices  11.9 us (3%)
    reduce_scatter x1, waiting for transfers between devices, shards(): lax.psum_scatter(key_partial.astype(jnp.bfloat16), 'blk', scatter_dimensi...  41.3 us
    all_to_all x1, blocking collectives, shards(): lax.all_to_all(projected[1:], 'head', split_axis=1, concat_axis=3, tiled=...  39.6 us
    all_gather x1, waiting for transfers between devices, shards(): key_all = lax.all_gather(key_vals, 'blk', axis=3, tiled=True)  34.5 us
    scatter-add x4, other arithmetic, backward_step(): grad_keys = grad_keys.at[chosen].add(d_keys)  28.4 us
    scatter-add x4, other arithmetic, backward_step(): grad_values = grad_values.at[chosen].add(d_values)  28.3 us
    dot_general x4, matrix products, forward_step(): jnp.einsum('hgbkc,gkhec->hegb', terms[6], terms[3], preferred_element_typ...  28.3 us
    gather x8, local copies, waits for them, and re-layouts, gather_group(): value_group = jnp.take(value_table, chosen, axis=0)  22.3 us
    gather x8, local copies, waits for them, and re-layouts, gather_group(): key_group = jnp.take(key_table, chosen, axis=0)  22.3 us
  transfers between devices with their start and end apart: 4, of which 4 were waited for; matrix products, arithmetic and copies ran while one was open for 1% of the time, Pallas kernels for 0%

commit v1 on v0

v1 whole, which is shorter than its diff:
```python
import functools
import math

import jax
import jax.numpy as jnp
from jax import lax
from jax.experimental import pallas as pl
from jax.experimental.pallas import tpu as pltpu
from jax.sharding import PartitionSpec as P

HEADS = 32
HEAD_DIM = 32
BLOCK = 128
SCALING = HEAD_DIM ** (-0.5)
epsilon = 1e-05


def dot_nt(a, b):
    return lax.dot_general(a, b, (((1,), (1,)), ((), ())), preferred_element_type=jnp.float32)


def spread_heads(block, heads):
    head_of = lax.broadcasted_iota(jnp.int32, block.shape, 1) // HEAD_DIM
    return jnp.concatenate(
        [jnp.where(head_of == h, block, jnp.zeros_like(block)) for h in range(heads)], axis=0
    )


def take_heads(wide, heads):
    return jnp.concatenate(
        [
            wide[h * HEAD_DIM : (h + 1) * HEAD_DIM, h * BLOCK : (h + 1) * BLOCK]
            for h in range(heads)
        ],
        axis=0,
    )


def forward_kernel(
    heads, slots, kb_ref, wt_ref, q_ref, kv_ref, posc_ref, posr_ref, o_ref, p_ref, g_ref
):
    i = pl.program_id(0)
    width = q_ref.shape[1]
    q_wide = spread_heads(q_ref[...], heads)
    pair = 2
    out_t = None
    for c in range(slots // pair):
        rows = [
            pl.ds(pl.multiple_of(kb_ref[i * slots + c * pair + s] * BLOCK, BLOCK), BLOCK)
            for s in range(pair)
        ]
        keys = jnp.concatenate([kv_ref[r, :width] for r in rows], axis=0)
        vals = jnp.concatenate([kv_ref[r, width:] for r in rows], axis=0)
        scores = dot_nt(keys, q_wide)
        probs = []
        for s in range(pair):
            weight = wt_ref[i * slots + c * pair + s]
            half = scores[s * BLOCK : (s + 1) * BLOCK, :] * (0.5 * SCALING)
            up = 1.0 + jnp.tanh(half)
            hu = half * up
            slope = up + hu * (2.0 - up)
            if c == 0 and s == 0:
                allowed = posc_ref[...] <= posr_ref[0]
                coefficient = jnp.where(allowed, weight, 0.0)
                coefficient = jnp.concatenate([coefficient] * heads, axis=1)
            else:
                coefficient = weight
            prob = (hu * coefficient).astype(jnp.bfloat16)
            at = (c * pair + s) * BLOCK
            p_ref[0, at : at + BLOCK, :] = prob
            g_ref[0, at : at + BLOCK, :] = (slope * (0.5 * coefficient)).astype(jnp.bfloat16)
            probs.append(prob)
        part = jnp.dot(vals.T, jnp.concatenate(probs, axis=0), preferred_element_type=jnp.float32)
        out_t = part if out_t is None else out_t + part
    o_ref[...] = take_heads(out_t, heads).T.astype(jnp.bfloat16)


def backward_kernel(
    heads, slots, kb_ref, q_ref, do_ref, kv_ref, p_ref, g_ref, dq_ref, dkv_ref, acc_ref
):
    i = pl.program_id(0)
    width = q_ref.shape[1]

    @pl.when(i == 0)
    def _():
        acc_ref[...] = jnp.zeros_like(acc_ref)

    q_wide = spread_heads(q_ref[...], heads)
    do_wide = spread_heads(do_ref[...], heads)
    pair = 2
    dq_t = None
    for c in range(slots // pair):
        rows = [
            pl.ds(pl.multiple_of(kb_ref[i * slots + c * pair + s] * BLOCK, BLOCK), BLOCK)
            for s in range(pair)
        ]
        keys = jnp.concatenate([kv_ref[r, :width] for r in rows], axis=0)
        vals = jnp.concatenate([kv_ref[r, width:] for r in rows], axis=0)
        at = c * pair * BLOCK
        prob = p_ref[0, at : at + pair * BLOCK, :]
        slope = g_ref[0, at : at + pair * BLOCK, :]
        d_scores = (dot_nt(vals, do_wide) * slope.astype(jnp.float32)).astype(jnp.bfloat16)
        d_vals = jnp.dot(prob, do_wide, preferred_element_type=jnp.float32)
        d_keys = jnp.dot(d_scores, q_wide, preferred_element_type=jnp.float32)
        part = jnp.dot(keys.T, d_scores, preferred_element_type=jnp.float32)
        dq_t = part if dq_t is None else dq_t + part
        for s in range(pair):
            acc_ref[rows[s], :width] += d_keys[s * BLOCK : (s + 1) * BLOCK, :]
            acc_ref[rows[s], width:] += d_vals[s * BLOCK : (s + 1) * BLOCK, :]
    dq_ref[...] = take_heads(dq_t, heads) * SCALING

    @pl.when(i == pl.num_programs(0) - 1)
    def _():
        dkv_ref[:, :width] = (acc_ref[:, :width] * SCALING).astype(jnp.bfloat16)
        dkv_ref[:, width:] = acc_ref[:, width:].astype(jnp.bfloat16)


def attention_forward(key_blocks, weights, query, key_vals, positions_here):
    local_blocks, slots = key_blocks.shape
    width = query.shape[1]
    heads = width // HEAD_DIM
    wide = heads * BLOCK
    whole = pl.BlockSpec(memory_space=pltpu.VMEM)
    smem = pl.BlockSpec(memory_space=pltpu.SMEM)
    stored = jax.ShapeDtypeStruct((local_blocks, slots * BLOCK, wide), jnp.bfloat16)
    return pl.pallas_call(
        functools.partial(forward_kernel, heads, slots),
        grid=(local_blocks,),
        in_specs=[
            smem,
            smem,
            pl.BlockSpec((BLOCK, width), lambda i: (i, 0)),
            whole,
            pl.BlockSpec((BLOCK, 1), lambda i: (i, 0)),
            pl.BlockSpec((1, 1, BLOCK), lambda i: (i, 0, 0)),
        ],
        out_specs=[
            pl.BlockSpec((BLOCK, width), lambda i: (i, 0)),
            pl.BlockSpec((1, slots * BLOCK, wide), lambda i: (i, 0, 0)),
            pl.BlockSpec((1, slots * BLOCK, wide), lambda i: (i, 0, 0)),
        ],
        out_shape=[jax.ShapeDtypeStruct(query.shape, jnp.bfloat16), stored, stored],
        compiler_params=pltpu.CompilerParams(vmem_limit_bytes=48 * 1024 * 1024),
        name="attention_forward",
    )(
        key_blocks.reshape(-1),
        weights.reshape(-1),
        query,
        key_vals,
        positions_here.reshape(-1, 1),
        positions_here.reshape(local_blocks, 1, BLOCK),
    )


def attention_backward(key_blocks, query, d_attended, key_vals, prob, slope):
    local_blocks, slots = key_blocks.shape
    width = query.shape[1]
    heads = width // HEAD_DIM
    wide = heads * BLOCK
    total = key_vals.shape[0]
    whole = pl.BlockSpec(memory_space=pltpu.VMEM)
    smem = pl.BlockSpec(memory_space=pltpu.SMEM)
    block = pl.BlockSpec((BLOCK, width), lambda i: (i, 0))
    stored = pl.BlockSpec((1, slots * BLOCK, wide), lambda i: (i, 0, 0))
    return pl.pallas_call(
        functools.partial(backward_kernel, heads, slots),
        grid=(local_blocks,),
        in_specs=[smem, block, block, whole, stored, stored],
        out_specs=[pl.BlockSpec((width, BLOCK), lambda i: (0, i)), whole],
        out_shape=[
            jax.ShapeDtypeStruct((width, query.shape[0]), jnp.float32),
            jax.ShapeDtypeStruct((total, 2 * width), jnp.bfloat16),
        ],
        scratch_shapes=[pltpu.VMEM((total, 2 * width), jnp.float32)],
        compiler_params=pltpu.CompilerParams(vmem_limit_bytes=48 * 1024 * 1024),
        name="attention_backward",
    )(key_blocks.reshape(-1), query, d_attended, key_vals, prob, slope)


def shards(tokens, w_proj, w_out, cotangent, key_blocks, exposures, positions):
    head_count = lax.axis_size("head")
    group_count = lax.axis_size("blk")
    segment_index = lax.axis_index("blk")
    local_rows, width = tokens.shape
    features = width // head_count
    segment = local_rows * head_count
    total_rows = segment * group_count
    projected = jax.nn.silu(
        jnp.dot(tokens, w_proj, preferred_element_type=jnp.float32)
    ).astype(jnp.bfloat16)
    gate_u = projected[:, :width].astype(jnp.float32)
    qkv = projected[:, width:].reshape(local_rows, 3, head_count, features)
    qkv = jnp.transpose(qkv, (2, 1, 0, 3))
    by_head = lax.all_to_all(qkv, "head", split_axis=0, concat_axis=0, tiled=True)
    query = by_head[:, 0].reshape(segment, features)
    key_vals = jnp.concatenate(
        [by_head[:, s].reshape(segment, features) for s in (1, 2)], axis=1
    )
    key_all = lax.all_gather(key_vals, "blk", axis=0, tiled=True)
    positions_here = lax.dynamic_slice_in_dim(positions, segment_index * segment, segment, 0)
    weights = jnp.log1p(exposures.astype(jnp.float32))
    attended, prob, slope = attention_forward(
        key_blocks, weights, query, key_all, positions_here
    )
    by_token = lax.all_to_all(attended, "head", split_axis=0, concat_axis=1, tiled=True)
    by_token = by_token.astype(jnp.float32)
    average = jnp.mean(by_token, axis=1, keepdims=True)
    centered = by_token - average
    variance = jnp.mean(centered * centered, axis=1, keepdims=True)
    inverse_std = lax.rsqrt(variance + epsilon)
    normed = centered * inverse_std
    gated = (normed * gate_u).astype(jnp.bfloat16)
    mixed = (
        tokens.astype(jnp.float32) + jnp.dot(gated, w_out, preferred_element_type=jnp.float32)
    ).astype(jnp.bfloat16)
    d_gated = dot_nt(cotangent, w_out)
    grad_u = (d_gated * normed).astype(jnp.bfloat16).T
    d_normed = d_gated * gate_u
    d_attended = inverse_std * (
        d_normed
        - jnp.mean(d_normed, axis=1, keepdims=True)
        - normed * jnp.mean(d_normed * normed, axis=1, keepdims=True)
    )
    d_heads = lax.all_to_all(
        d_attended.astype(jnp.bfloat16), "head", split_axis=1, concat_axis=0, tiled=True
    )
    grad_query, partial = attention_backward(
        key_blocks, query, d_heads, key_all, prob, slope
    )
    summed = lax.psum_scatter(partial, "blk", scatter_dimension=0, tiled=True)
    summed = summed.T.reshape(2, features, segment).astype(jnp.float32)
    grad_qkv = jnp.concatenate([grad_query[None], summed], axis=0)
    return (mixed, grad_u, grad_qkv)


def solution(mesh):
    in_specs = (
        P(("blk", "head"), None),
        P(),
        P(),
        P(("blk", "head"), None),
        P("blk", None),
        P("blk", None),
        P(),
    )
    out_specs = (P(("blk", "head"), None), P(None, ("blk", "head")), P(None, "head", "blk"))
    return jax.shard_map(shards, mesh=mesh, in_specs=in_specs, out_specs=out_specs, check_vma=False)
```

time: 468 us -> 253 us (0.54)
  local copies, waits for them, and re-layouts: 108 us -> 10.7 us
  other arithmetic: 96.8 us -> 9.06 us
  matrix products: 90.6 us -> 9.98 us
  Pallas kernels: 0 us -> 56.9 us
  blocking collectives: 39.6 us -> 74.2 us
  waiting for transfers between devices: 99.7 us -> 75.6 us
  starting transfers between devices: 11.9 us -> 0.08 us
    dot_general x27 -> x3, matrix products: 90.6 us -> 9.98 us  [the longest x1 6.15 us: shards(): jnp.dot(tokens, w_proj, preferred_element_type=jnp.float32)]
    pallas_call x0 -> x2, Pallas kernels: none -> 56.9 us  [the longest x1 29.1 us: attention_forward(): pl.pallas_call(functools.partial(forward_kernel, heads, slots), grid=(loc...]
    scatter-add x8 -> x0, other arithmetic: 56.7 us -> none  [the longest x4 28.4 us: backward_step(): grad_keys = grad_keys.at[chosen].add(d_keys)]
    gather x24 -> x0, local copies, waits for them, and re-layouts: 49.2 us -> none  [the longest x8 22.3 us: gather_group(): value_group = jnp.take(value_table, chosen, axis=0)]
    all_to_all x1 -> x3, blocking collectives: 39.6 us -> 74.2 us  [the longest x1 39.4 us: shards(): lax.all_to_all(qkv, 'head', split_axis=0, concat_axis=0, tiled=True)]
    all_to_all x2 -> x0, waiting for transfers between devices: 23.9 us -> none  [the longest x1 12 us: shards(): lax.all_to_all(attended, 'head', split_axis=2, concat_axis=0, tiled=True)]
    reduce_sum x3 -> x2, other arithmetic: 17.9 us -> 0.43 us  [the longest x1 0.28 us: shards(): variance = jnp.mean(centered * centered, axis=1, keepdims=True)]
    all_to_all x2 -> x0, starting transfers between devices: 11.8 us -> none  [the longest x1 6.35 us: shards(): lax.all_to_all(d_attended, 'head', split_axis=0, concat_axis=2, tiled=True)]
  transfers between devices with their start and end apart: 4 -> 2, of which waited for: 4 -> 2; matrix products, arithmetic and copies ran while one was open for 1% -> 2% of each run, Pallas kernels for 0% -> 0%
where the time goes in v1:
time: 253 us; the launch traced here: 251 us
  waiting for transfers between devices  75.6 us (30%)
  blocking collectives  74.2 us (29%)
  Pallas kernels  56.9 us (22%)
  between operations  14.2 us (6%)
  local copies, waits for them, and re-layouts  10.7 us (4%)
  matrix products  9.98 us (4%)
  other arithmetic  9.06 us (4%)
    reduce_scatter x1, waiting for transfers between devices, shards(): summed = lax.psum_scatter(partial, 'blk', scatter_dimension=0, tiled=True)  41 us
    all_to_all x1, blocking collectives, shards(): lax.all_to_all(qkv, 'head', split_axis=0, concat_axis=0, tiled=True)  39.4 us
    all_gather x1, waiting for transfers between devices, shards(): key_all = lax.all_gather(key_vals, 'blk', axis=0, tiled=True)  34.6 us
    pallas_call x1, Pallas kernels, attention_forward(): pl.pallas_call(functools.partial(forward_kernel, heads, slots), grid=(loc...  29.1 us
    pallas_call x1, Pallas kernels, attention_backward(): pl.pallas_call(functools.partial(backward_kernel, heads, slots), grid=(lo...  27.8 us
    all_to_all x1, blocking collectives, shards(): lax.all_to_all(d_attended.astype(jnp.bfloat16), 'head', split_axis=1, con...  17.7 us
    all_to_all x1, blocking collectives, shards(): lax.all_to_all(attended, 'head', split_axis=0, concat_axis=1, tiled=True)  17 us
    dot_general x1, matrix products, shards(): jnp.dot(tokens, w_proj, preferred_element_type=jnp.float32)  6.15 us
  transfers between devices with their start and end apart: 2, of which 2 were waited for; matrix products, arithmetic and copies ran while one was open for 2% of the time, Pallas kernels for 0%

profile of v1, /device:TPU:11, one launch (start us, length us, event | category | flops | bytes accessed | tf_op | source)
XLA Modules:
  0.0 250.7 jit_solution(8242517062119342426)
XLA Ops:
  7.2 6.1 %multiply_convert_fusion = bf16[256,4096]{1,0:T(8,128)(2,1)S(1)} fusion(bf16[256,1024]{1,0:T(8,128)(2,1)} %param.7, bf16[1024,4096]{1,0:T(8,128)(2,1)} %param.8), kind=kOutput, calls=%fused_computation | convolution fusion | flops 2152726528 | bytes 11010048 | tf_op jit(solution)/shard_map/dot_general | solution.py:189
  13.5 0.3 copy.36
  13.8 0.3 copy.49
  14.2 39.4 %all_to_all.37 = bf16[8,3,256,128]{3,2,1,0:T(8,128)(2,1)S(1)} all-to-all(bf16[8,3,256,128]{3,2,1,0:T(8,128)(2,1)S(1)} %bitcast.61), channel_id=1, replica_groups=mesh['head'=8,'blk'=4] {'head'}, dimensions={0} | all-to-all | bytes 3145728 | tf_op jit(solution)/shard_map/all_to_all | solution.py:194
  53.8 1.1 pad_maximum_fusion.1
  55.3 0.7 dynamic_slice.3
  56.0 1.4 copy.28.posc_ref
  57.4 34.6 %all-gather.2.cloned.1.call-done.kv_ref = bf16[8192,256]{1,0:T(8,128)(2,1)} async-done(((bf16[2048,256]{1,0:T(8,128)(2,1)}), bf16[8192,256]{1,0:T(8,128)(2,1)}) %all-gather.2.cloned.1.call-update) | async-done | bytes 4194320 | tf_op jit(solution)/shard_map/all_gather | solution.py:199
  92.0 1.2 copy-done.1
  93.3 29.1 %attention_forward.1 = (bf16[2048,128]{1,0:T(8,128)(2,1)S(1)}, bf16[16,1024,512]{2,1,0:T(8,128)(2,1)}, bf16[16,1024,512]{2,1,0:T(8,128)(2,1)}) custom-call(s32[128]{0:T(128)S(1)} %reshape.58.kb_ref, f32[128]{0:T(128)S(1)} %reshape.59.wt_ref, bf16[2048,128]{1,0:T(8,128)(2,1)S(1)} %bitcast.52, bf16[8192,256]{1,0:T(8,128)(2,1)} %all-gather.2.cloned.1.call-done.kv_ref, ...), custom_call_target="tpu_custom_call" | custom-call | tf_op jit(solution)/shard_map/attention_forward/pallas_call | solution.py:126
  122.4 17.0 %all_to_all.38 = bf16[8,256,128]{2,1,0:T(8,128)(2,1)S(1)} all-to-all(bf16[8,256,128]{2,1,0:T(8,128)(2,1)S(1)} %bitcast.56), channel_id=1, replica_groups=mesh['head'=8,'blk'=4] {'head'}, dimensions={0} | all-to-all | bytes 1048576 | tf_op jit(solution)/shard_map/all_to_all | solution.py:205
  139.6 0.3 fusion.3
  139.9 1.0 fusion.9
  140.9 1.3 fusion.6
  142.3 17.7 %all_to_all.39 = bf16[256,8,128]{2,0,1:T(8,128)(2,1)S(1)} all-to-all(bf16[256,8,128]{2,0,1:T(8,128)(2,1)S(1)} %bitcast.62), channel_id=1, replica_groups=mesh['head'=8,'blk'=4] {'head'}, dimensions={1} | all-to-all | bytes 1048576 | tf_op jit(solution)/shard_map/all_to_all | solution.py:224
  160.0 27.8 %attention_backward.1 = (f32[128,2048]{1,0:T(8,128)S(1)}, bf16[8192,256]{1,0:T(8,128)(2,1)}) custom-call(s32[128]{0:T(128)S(1)} %reshape.58.kb_ref, bf16[2048,128]{1,0:T(8,128)(2,1)S(1)} %bitcast.53, bf16[2048,128]{1,0:T(8,128)(2,1)S(1)} %bitcast.54, bf16[8192,256]{1,0:T(8,128)(2,1)} %all-gather.2.cloned.1.call-done.kv_ref, ...), custom_call_target="tpu_custom_call" | custom-call | tf_op jit(solution)/shard_map/attention_backward/pallas_call | solution.py:165
  187.8 1.0 copy-done.2
  188.8 1.0 copy-done.6
  189.8 1.0 copy.32
  190.8 2.8 %fusion = bf16[256,1024]{1,0:T(8,128)(2,1)} fusion(bf16[1024,1024]{1,0:T(8,128)(2,1)S(1)} %copy-done, bf16[256,1024]{1,0:T(8,128)(2,1)} %param.7, bf16[256,4096]{1,0:T(8,128)(2,1)} %copy-done.4, f32[256]{0:T(256)S(1)} %add_rsqrt_fusion, f32[256]{0:T(256)S(1)} %broadcast_multiply_fusion.2, bf16[8,256,128]{2,1,0:T(8,128)(2,1)S(1)} %all_to_all.38), kind=kOutput, calls=%fused_computation.11 | convolution fusion | flops 539230208 | bytes 4196352 | tf_op jit(solution)/shard_map/dot_general | solution.py:214
  193.6 41.0 %reduce-scatter.2.cloned.1.call-done = bf16[2048,256]{1,0:T(8,128)(2,1)} async-done(((bf16[8192,256]{1,0:T(8,128)(2,1)}), bf16[2048,256]{1,0:T(8,128)(2,1)}) %reduce-scatter.2.cloned.1.call-update) | async-done | bytes 1048592 | tf_op jit(solution)/shard_map/reduce_scatter | solution.py:230
  234.6 2.7 %convert_bitcast_fusion = f32[256,2048]{0,1:T(8,128)} fusion(bf16[2048,256]{1,0:T(8,128)(2,1)} %reduce-scatter.2.cloned.1.call-done), kind=kLoop, calls=%fused_computation.2 | loop fusion | flops 524288 | bytes 3145728 | tf_op jit(solution)/shard_map/convert_element_type | solution.py:231
  237.3 3.0 %copy.33 = f32[256,2048]{1,0:T(8,128)} copy(f32[256,2048]{0,1:T(8,128)} %convert_bitcast_fusion) | data formatting | bytes 4194304 | tf_op jit(solution)/shard_map/convert_element_type | solution.py:231
  240.3 3.6 %pad_maximum_fusion = f32[3,128,2048]{2,1,0:T(8,128)} fusion(f32[2,128,2048]{2,1,0:T(8,128)} %bitcast.59, f32[1,128,2048]{2,1,0:T(8,128)S(1)} %bitcast.55), kind=kLoop, calls=%fused_computation.1 | loop fusion | flops 786432 | bytes 6291456 | tf_op jit(solution)/shard_map/concatenate | solution.py:232
  (33 shorter events, 1.0 us)
Async XLA Ops:
  7.2 132.7 %copy-start = (bf16[1024,1024]{1,0:T(8,128)(2,1)S(1)}, bf16[1024,1024]{1,0:T(8,128)(2,1)}, u32[]{:S(2)}) copy-start(bf16[1024,1024]{1,0:T(8,128)(2,1)} %param.9) | copy-start | bytes 6291460
  7.2 84.9 %all-gather.2.cloned.1.call-start = ((), (), s32[]{:S(2)}) async-start(), calls=%async_computation.4 | async-start | bytes 5242880 | tf_op jit(solution)/shard_map/all_gather | solution.py:199
  13.4 40.2 %copy-start.4 = (bf16[256,4096]{1,0:T(8,128)(2,1)}, bf16[256,4096]{1,0:T(8,128)(2,1)S(1)}, u32[]{:S(2)}) copy-start(bf16[256,4096]{1,0:T(8,128)(2,1)S(1)} %multiply_convert_fusion) | copy-start | bytes 6291460
  53.8 1.2 copy-start.8
  53.8 1.4 copy-start.7
  54.9 179.7 %reduce-scatter.2.cloned.1.call-start = ((), (), s32[]{:S(2)}) async-start(), calls=%async_computation.5 | async-start | bytes 5242880 | tf_op jit(solution)/shard_map/reduce_scatter | solution.py:230
  92.0 1.2 copy-start.1
  93.3 46.6 %copy-start.9 = (bf16[256,1024]{1,0:T(8,128)(2,1)S(1)}, bf16[256,1024]{1,0:T(8,128)(2,1)}, u32[]{:S(2)}) copy-start(bf16[256,1024]{1,0:T(8,128)(2,1)} %param.10) | copy-start | bytes 1572868
  122.4 17.5 %copy-start.5 = (bf16[256,4096]{1,0:T(8,128)(2,1)S(1)}, bf16[256,4096]{1,0:T(8,128)(2,1)}, u32[]{:S(2)}) copy-start(bf16[256,4096]{1,0:T(8,128)(2,1)} %copy-done.4) | copy-start | bytes 6291460
  187.8 1.0 copy-start.2
  188.8 1.0 copy-start.6
  237.3 3.0 %copy-start.3 = (f32[128,2048]{1,0:T(8,128)S(1)}, f32[128,2048]{1,0:T(8,128)}, u32[]{:S(2)}) copy-start(f32[128,2048]{1,0:T(8,128)} %copy-done.2) | copy-start | bytes 3145732
Sparse Core Ops, SparseCore 0:
  55.0 36.9 all-gather.1
  188.9 45.6 reduce-scatter.1

commit v2 on v1

--- a/solution.py
+++ b/solution.py
@@ -1,5 +1,4 @@
 import functools
-import math
 
 import jax
 import jax.numpy as jnp
@@ -177,6 +176,219 @@
     )(key_blocks.reshape(-1), query, d_attended, key_vals, prob, slope)
 
 
+def greet(peers):
+    barrier = pltpu.get_barrier_semaphore()
+    for peer in peers:
+        pl.semaphore_signal(
+            barrier, inc=1, device_id=peer, device_id_type=pl.DeviceIdType.MESH
+        )
+    pl.semaphore_wait(barrier, len(peers))
+
+
+def send(source, target, send_sem, recv_sem, peer):
+    copy = pltpu.make_async_remote_copy(
+        src_ref=source,
+        dst_ref=target,
+        send_sem=send_sem,
+        recv_sem=recv_sem,
+        device_id=peer,
+        device_id_type=pl.DeviceIdType.MESH,
+    )
+    copy.start()
+    return copy
+
+
+def blk_partners(here):
+    return here + 1 - 2 * lax.rem(here, 2), lax.rem(here + 2, 4)
+
+
+def exchange_kernel(count, x_ref, o_ref, local_sem, send_sem, recv_sem):
+    me = lax.axis_index("head")
+    others = [lax.rem(me + k, count) for k in range(1, count)]
+    greet([{"head": other} for other in others])
+    local = pltpu.make_async_copy(x_ref.at[me], o_ref.at[me], local_sem)
+    local.start()
+    copies = [
+        send(x_ref.at[other], o_ref.at[me], send_sem.at[k], recv_sem.at[k], {"head": other})
+        for k, other in enumerate(others)
+    ]
+    local.wait()
+    for copy in copies:
+        copy.wait()
+
+
+def exchange(x, collective_id):
+    count = x.shape[0]
+    anywhere = pl.BlockSpec(memory_space=pl.ANY)
+    return pl.pallas_call(
+        functools.partial(exchange_kernel, count),
+        in_specs=[anywhere],
+        out_specs=anywhere,
+        out_shape=jax.ShapeDtypeStruct(x.shape, x.dtype),
+        scratch_shapes=[
+            pltpu.SemaphoreType.DMA,
+            pltpu.SemaphoreType.DMA((count - 1,)),
+            pltpu.SemaphoreType.DMA((count - 1,)),
+        ],
+        compiler_params=pltpu.CompilerParams(collective_id=collective_id, has_side_effects=True),
+        name="exchange",
+    )(x)
+
+
+def distribute_kernel(
+    count, kv_ref, q_ref, kv_out, q_out, local_sem, kv_sem, q_sem, side_sem, core_sem, pass_sem
+):
+    me, here = lax.axis_index("head"), lax.axis_index("blk")
+    core, side = blk_partners(here)
+    rows = kv_ref.shape[1]
+    others = [lax.rem(me + k, count) for k in range(1, count)]
+    greet([{"head": other} for other in others] + [{"blk": core}, {"blk": side}])
+
+    def place(segment, source):
+        start = pl.multiple_of((segment * count + source) * rows, rows)
+        return kv_out.at[pl.ds(start, rows), :]
+
+    local_kv = pltpu.make_async_copy(kv_ref.at[me], place(here, me), local_sem.at[0])
+    local_kv.start()
+    local_q = pltpu.make_async_copy(q_ref.at[me], q_out.at[me], local_sem.at[1])
+    local_q.start()
+    kv_copies = [
+        send(
+            kv_ref.at[other],
+            place(here, me),
+            kv_sem.at[0, k],
+            kv_sem.at[1, k],
+            {"head": other},
+        )
+        for k, other in enumerate(others)
+    ]
+    q_copies = [
+        send(q_ref.at[other], q_out.at[me], q_sem.at[0, k], q_sem.at[1, k], {"head": other})
+        for k, other in enumerate(others)
+    ]
+    side_copies, core_copies, pass_copies = [], [], []
+    lag = 2
+    for k in range(count + lag):
+        if k < count:
+            if k == 0:
+                local_kv.wait()
+            else:
+                kv_copies[k - 1].wait_recv()
+            chunk = place(here, lax.rem(me - k + count, count))
+            side_copies.append(
+                send(chunk, chunk, side_sem.at[0, k], side_sem.at[1, k], {"blk": side})
+            )
+            core_copies.append(
+                send(chunk, chunk, core_sem.at[0, k], core_sem.at[1, k], {"blk": core})
+            )
+        j = k - lag
+        if j >= 0:
+            side_copies[j].wait_recv()
+            chunk = place(side, lax.rem(me - j + count, count))
+            pass_copies.append(
+                send(chunk, chunk, pass_sem.at[0, j], pass_sem.at[1, j], {"blk": core})
+            )
+    local_q.wait()
+    for copy in kv_copies + side_copies:
+        copy.wait_send()
+    for copy in q_copies + core_copies + pass_copies:
+        copy.wait()
+
+
+def distribute(kv, q, groups):
+    count, rows, width = kv.shape
+    anywhere = pl.BlockSpec(memory_space=pl.ANY)
+    pair = pltpu.SemaphoreType.DMA((2, count))
+    return pl.pallas_call(
+        functools.partial(distribute_kernel, count),
+        in_specs=[anywhere, anywhere],
+        out_specs=[anywhere, anywhere],
+        out_shape=[
+            jax.ShapeDtypeStruct((groups * count * rows, width), kv.dtype),
+            jax.ShapeDtypeStruct(q.shape, q.dtype),
+        ],
+        scratch_shapes=[pltpu.SemaphoreType.DMA((2,)), pair, pair, pair, pair, pair],
+        compiler_params=pltpu.CompilerParams(collective_id=0, has_side_effects=True),
+        name="distribute",
+    )(kv, q)
+
+
+def collect_kernel(
+    chunks, part_ref, dq_ref, o_ref, core_in, side_out, side_in, near_sem, far_sem, side_sem
+):
+    here = lax.axis_index("blk")
+    core, side = blk_partners(here)
+    far = lax.rem(core + 2, 4)
+    width, segment = dq_ref.shape
+    rows = segment // chunks
+    greet([{"blk": core}, {"blk": side}])
+    far_copies = [
+        send(
+            part_ref.at[far, c], core_in.at[1, c], far_sem.at[0, c], far_sem.at[1, c], {"blk": core}
+        )
+        for c in range(chunks)
+    ]
+    near_copies = [
+        send(
+            part_ref.at[core, c],
+            core_in.at[0, c],
+            near_sem.at[0, c],
+            near_sem.at[1, c],
+            {"blk": core},
+        )
+        for c in range(chunks)
+    ]
+    side_copies = []
+    for c in range(chunks):
+        far_copies[c].wait_recv()
+        total = part_ref[side, c].astype(jnp.float32) + core_in[1, c].astype(jnp.float32)
+        side_out[c] = total.astype(jnp.bfloat16)
+        side_copies.append(
+            send(
+                side_out.at[c], side_in.at[c], side_sem.at[0, c], side_sem.at[1, c], {"blk": side}
+            )
+        )
+    o_ref[:width, :] = dq_ref[...]
+    for c in range(chunks):
+        near_copies[c].wait_recv()
+        side_copies[c].wait_recv()
+        total = (
+            part_ref[here, c].astype(jnp.float32)
+            + core_in[0, c].astype(jnp.float32)
+            + side_in[c].astype(jnp.float32)
+        )
+        o_ref[width:, c * rows : (c + 1) * rows] = total.T
+    for copy in far_copies + near_copies + side_copies:
+        copy.wait_send()
+
+
+def collect(partial, grad_query, groups):
+    width, segment = grad_query.shape
+    chunks = 8
+    rows = segment // chunks
+    vmem = pl.BlockSpec(memory_space=pltpu.VMEM)
+    pair = pltpu.SemaphoreType.DMA((2, chunks))
+    block = (chunks, rows, 2 * width)
+    return pl.pallas_call(
+        functools.partial(collect_kernel, chunks),
+        in_specs=[vmem, vmem],
+        out_specs=vmem,
+        out_shape=jax.ShapeDtypeStruct((3 * width, segment), jnp.float32),
+        scratch_shapes=[
+            pltpu.VMEM((2,) + block, jnp.bfloat16),
+            pltpu.VMEM(block, jnp.bfloat16),
+            pltpu.VMEM(block, jnp.bfloat16),
+            pair,
+            pair,
+            pair,
+        ],
+        compiler_params=pltpu.CompilerParams(
+            collective_id=3, has_side_effects=True, vmem_limit_bytes=48 * 1024 * 1024
+        ),
+        name="collect",
+    )(partial.reshape((groups,) + block), grad_query)
+
+
 def shards(tokens, w_proj, w_out, cotangent, key_blocks, exposures, positions):
     head_count = lax.axis_size("head")
     group_count = lax.axis_size("blk")
@@ -184,25 +396,25 @@
     local_rows, width = tokens.shape
     features = width // head_count
     segment = local_rows * head_count
-    total_rows = segment * group_count
     projected = jax.nn.silu(
         jnp.dot(tokens, w_proj, preferred_element_type=jnp.float32)
     ).astype(jnp.bfloat16)
     gate_u = projected[:, :width].astype(jnp.float32)
-    qkv = projected[:, width:].reshape(local_rows, 3, head_count, features)
-    qkv = jnp.transpose(qkv, (2, 1, 0, 3))
-    by_head = lax.all_to_all(qkv, "head", split_axis=0, concat_axis=0, tiled=True)
-    query = by_head[:, 0].reshape(segment, features)
-    key_vals = jnp.concatenate(
-        [by_head[:, s].reshape(segment, features) for s in (1, 2)], axis=1
-    )
-    key_all = lax.all_gather(key_vals, "blk", axis=0, tiled=True)
+    by_owner = projected[:, width:].reshape(local_rows, 3, head_count, features)
+    key_vals = jnp.concatenate([by_owner[:, 1], by_owner[:, 2]], axis=2)
+    key_all, query = distribute(
+        jnp.transpose(key_vals, (1, 0, 2)),
+        jnp.transpose(by_owner[:, 0], (1, 0, 2)),
+        group_count,
+    )
+    query = query.reshape(segment, features)
     positions_here = lax.dynamic_slice_in_dim(positions, segment_index * segment, segment, 0)
     weights = jnp.log1p(exposures.astype(jnp.float32))
     attended, prob, slope = attention_forward(
         key_blocks, weights, query, key_all, positions_here
     )
-    by_token = lax.all_to_all(attended, "head", split_axis=0, concat_axis=1, tiled=True)
+    by_token = exchange(attended.reshape(head_count, local_rows, features), 1)
+    by_token = jnp.transpose(by_token, (1, 0, 2)).reshape(local_rows, width)
     by_token = by_token.astype(jnp.float32)
     average = jnp.mean(by_token, axis=1, keepdims=True)
     centered = by_token - average
@@ -221,15 +433,12 @@
         - jnp.mean(d_normed, axis=1, keepdims=True)
         - normed * jnp.mean(d_normed * normed, axis=1, keepdims=True)
     )
-    d_heads = lax.all_to_all(
-        d_attended.astype(jnp.bfloat16), "head", split_axis=1, concat_axis=0, tiled=True
-    )
+    d_attended = d_attended.astype(jnp.bfloat16).reshape(local_rows, head_count, features)
+    d_heads = exchange(jnp.transpose(d_attended, (1, 0, 2)), 2).reshape(segment, features)
     grad_query, partial = attention_backward(
         key_blocks, query, d_heads, key_all, prob, slope
     )
-    summed = lax.psum_scatter(partial, "blk", scatter_dimension=0, tiled=True)
-    summed = summed.T.reshape(2, features, segment).astype(jnp.float32)
-    grad_qkv = jnp.concatenate([grad_query[None], summed], axis=0)
+    grad_qkv = collect(partial, grad_query, group_count).reshape(3, features, segment)
     return (mixed, grad_u, grad_qkv)
 
 

time: 253 us -> 214 us (0.85)
  Pallas kernels: 56.9 us -> 165 us
  waiting for transfers between devices: 75.6 us -> 0 us
  blocking collectives: 74.2 us -> 0 us
  local copies, waits for them, and re-layouts: 10.7 us -> 29.5 us
  between operations: 14.2 us -> 0.8 us
    pallas_call x0 -> x4, Pallas kernels: none -> 108 us  [the longest x1 42.6 us: distribute(): pl.pallas_call(functools.partial(distribute_kernel, count), in_specs=[any...]
    all_to_all x3 -> x0, blocking collectives: 74.2 us -> none  [the longest x1 39.4 us: shards(): lax.all_to_all(qkv, 'head', split_axis=0, concat_axis=0, tiled=True)]
    reduce_scatter x1 -> x0, waiting for transfers between devices: 41 us -> none  [shards(): summed = lax.psum_scatter(partial, 'blk', scatter_dimension=0, tiled=True)]
    all_gather x1 -> x0, waiting for transfers between devices: 34.6 us -> none  [shards(): key_all = lax.all_gather(key_vals, 'blk', axis=0, tiled=True)]
    unnamed x24 -> x28, local copies, waits for them, and re-layouts: 4.77 us -> 17.7 us
    slice x1 -> x3, local copies, waits for them, and re-layouts: 0.13 us -> 6.42 us  [the longest x2 3.88 us: shards(): by_owner = projected[:, width:].reshape(local_rows, 3, head_count, features)]
    concatenate x2 -> x0, other arithmetic: 4.64 us -> none  [the longest x1 3.56 us: shards(): grad_qkv = jnp.concatenate([grad_query[None], summed], axis=0)]
  transfers between devices with their start and end apart: 2 -> 0, of which waited for: 2 -> 0; matrix products, arithmetic and copies ran while one was open for 2% -> 0% of each run, Pallas kernels for 0% -> 0%
where the time goes in v2:
time: 214 us; the launch traced here: 213 us
  Pallas kernels  165 us (77%)
  local copies, waits for them, and re-layouts  29.5 us (14%)
  matrix products  10 us (5%)
  other arithmetic  7.99 us (4%)
    pallas_call x1, Pallas kernels, distribute(): pl.pallas_call(functools.partial(distribute_kernel, count), in_specs=[any...  42.6 us
    pallas_call x2, Pallas kernels, exchange(): pl.pallas_call(functools.partial(exchange_kernel, count), in_specs=[anywh...  35.8 us
    pallas_call x1, Pallas kernels, collect(): pl.pallas_call(functools.partial(collect_kernel, chunks), in_specs=[vmem,...  29.6 us
    pallas_call x1, Pallas kernels, attention_forward(): pl.pallas_call(functools.partial(forward_kernel, heads, slots), grid=(loc...  29.1 us
    pallas_call x1, Pallas kernels, attention_backward(): pl.pallas_call(functools.partial(backward_kernel, heads, slots), grid=(lo...  27.8 us
    unnamed x28, local copies, waits for them, and re-layouts  17.7 us
    dot_general x1, matrix products, shards(): jnp.dot(tokens, w_proj, preferred_element_type=jnp.float32)  6.04 us

profile of v2, /device:TPU:11, one launch (start us, length us, event | category | flops | bytes accessed | tf_op | source)
XLA Modules:
  0.0 213.1 jit_solution(8065670614621035394)
XLA Ops:
  3.6 6.0 %multiply_convert_fusion = bf16[256,4096]{1,0:T(8,128)(2,1)S(1)} fusion(bf16[256,1024]{1,0:T(8,128)(2,1)} %param.7, bf16[1024,4096]{1,0:T(8,128)(2,1)} %param.8), kind=kOutput, calls=%fused_computation | convolution fusion | flops 2152726528 | bytes 11010048 | tf_op jit(solution)/shard_map/dot_general | solution.py:400
  9.6 1.3 copy-done.7
  11.0 1.3 slice.20
  12.3 2.6 %copy.15 = bf16[256,3072]{0,1:T(8,128)(2,1)} copy(bf16[256,3072]{1,0:T(8,128)(2,1)} %slice.20) | data formatting | bytes 3145728 | tf_op jit(solution)/shard_map/slice | solution.py:403
  14.8 2.5 %fusion.10 = (bf16[256,1,8,128]{0,3,2,1:T(8,128)(2,1)}, bf16[256,1,8,128]{0,3,2,1:T(8,128)(2,1)}, bf16[256,1,8,128]{0,3,2,1:T(8,128)(2,1)}) fusion(bf16[256,3,8,128]{0,3,2,1:T(8,128)(2,1)} %bitcast.34), kind=kLoop, calls=%fused_computation.26 | loop fusion | bytes 3145728 | tf_op jit(solution)/shard_map/slice | solution.py:407
  17.4 2.1 copy.27
  19.4 2.0 copy.26
  21.5 2.0 copy.25
  23.5 2.3 %maximum_bitcast_fusion.kv_ref = bf16[8,256,256]{2,1,0:T(8,128)(2,1)} fusion(bf16[256,8,128]{2,0,1:T(8,128)(2,1)} %bitcast.40, bf16[256,8,128]{2,0,1:T(8,128)(2,1)} %bitcast.41), kind=kLoop, calls=%fused_computation.11 | loop fusion | flops 2097152 | bytes 2097152 | tf_op jit(solution)/shard_map/transpose | solution.py:406
  25.8 42.6 %distribute.1 = (bf16[8192,256]{1,0:T(8,128)(2,1)}, bf16[8,256,128]{2,1,0:T(8,128)(2,1)}) custom-call(bf16[8,256,256]{2,1,0:T(8,128)(2,1)} %maximum_bitcast_fusion.kv_ref, bf16[8,256,128]{2,1,0:T(8,128)(2,1)} %bitcast.37), custom_call_target="tpu_custom_call" | custom-call | tf_op jit(solution)/shard_map/distribute/pallas_call | solution.py:302
  69.4 29.1 %attention_forward.1 = (bf16[2048,128]{1,0:T(8,128)(2,1)S(1)}, bf16[16,1024,512]{2,1,0:T(8,128)(2,1)}, bf16[16,1024,512]{2,1,0:T(8,128)(2,1)}) custom-call(s32[128]{0:T(128)S(1)} %reshape.68.kb_ref, f32[128]{0:T(128)S(1)} %reshape.69.wt_ref, bf16[2048,128]{1,0:T(8,128)(2,1)S(1)} %bitcast.28, bf16[8192,256]{1,0:T(8,128)(2,1)} %get-tuple-element.11.kv_ref, ...), custom_call_target="tpu_custom_call" | custom-call | tf_op jit(solution)/shard_map/attention_forward/pallas_call | solution.py:125
  99.3 21.1 %exchange.2 = bf16[8,256,128]{2,1,0:T(8,128)(2,1)} custom-call(bf16[8,256,128]{2,1,0:T(8,128)(2,1)} %bitcast.31), custom_call_target="tpu_custom_call" | custom-call | tf_op jit(solution)/shard_map/exchange/pallas_call | solution.py:223
  120.4 1.2 convert_reduce_fusion
  121.6 1.3 fusion.3
  122.9 1.1 convert_bitcast_fusion
  124.1 1.3 copy.20
  125.4 1.6 copy.21
  127.0 3.0 %fusion = bf16[256,1024]{1,0:T(8,128)(2,1)} fusion(bf16[1024,1024]{1,0:T(8,128)(2,1)S(1)} %copy-done, bf16[256,1024]{1,0:T(8,128)(2,1)} %param.7, f32[256,1024]{1,0:T(8,128)S(1)} %copy.21, f32[256]{0:T(256)S(1)} %add_rsqrt_fusion, f32[256]{0:T(256)S(1)} %broadcast_multiply_fusion.2, bf16[256,4096]{1,0:T(8,128)(2,1)} %copy-done.7), kind=kOutput, calls=%fused_computation.7 | convolution fusion | flops 538968064 | bytes 4720640 | tf_op jit(solution)/shard_map/dot_general | solution.py:426
  131.0 1.2 multiply_convert_fusion.1
  133.4 14.7 %exchange.3 = bf16[8,256,128]{2,1,0:T(8,128)(2,1)} custom-call(bf16[8,256,128]{2,1,0:T(8,128)(2,1)} %bitcast.39), custom_call_target="tpu_custom_call" | custom-call | tf_op jit(solution)/shard_map/exchange/pallas_call | solution.py:223
  149.1 27.8 %attention_backward.1 = (f32[128,2048]{1,0:T(8,128)S(1)}, bf16[8192,256]{1,0:T(8,128)(2,1)}) custom-call(s32[128]{0:T(128)S(1)} %reshape.68.kb_ref, bf16[2048,128]{1,0:T(8,128)(2,1)S(1)} %bitcast.29, bf16[2048,128]{1,0:T(8,128)(2,1)S(1)} %bitcast.30, bf16[8192,256]{1,0:T(8,128)(2,1)} %get-tuple-element.11.kv_ref, ...), custom_call_target="tpu_custom_call" | custom-call | tf_op jit(solution)/shard_map/attention_backward/pallas_call | solution.py:164
  176.9 29.6 %collect.1 = f32[384,2048]{1,0:T(8,128)S(1)} custom-call(bf16[4,8,256,256]{3,2,1,0:T(8,128)(2,1)} %bitcast.35, f32[128,2048]{1,0:T(8,128)S(1)} %get-tuple-element.16.dq_ref), custom_call_target="tpu_custom_call" | custom-call | tf_op jit(solution)/shard_map/collect/pallas_call | solution.py:372
  206.6 1.6 copy-done.2
  209.2 3.9 %copy.29 = f32[3,128,2048]{2,1,0:T(8,128)} copy(f32[3,128,2048]{2,1,0:T(8,128)} %bitcast.27) | data formatting | bytes 6291456
  (34 shorter events, 9.0 us)
Async XLA Ops:
  0.6 126.3 %copy-start = (bf16[1024,1024]{1,0:T(8,128)(2,1)S(1)}, bf16[1024,1024]{1,0:T(8,128)(2,1)}, u32[]{:S(2)}) copy-start(bf16[1024,1024]{1,0:T(8,128)(2,1)} %param.9) | copy-start | bytes 6291460
  9.6 1.3 copy-start.7
  68.4 1.0 copy-start.3
  98.5 0.8 copy-start.6
  127.0 3.0 %copy-start.8 = (bf16[256,4096]{1,0:T(8,128)(2,1)S(1)}, bf16[256,4096]{1,0:T(8,128)(2,1)}, u32[]{:S(2)}) copy-start(bf16[256,4096]{1,0:T(8,128)(2,1)} %copy-done.7) | copy-start | bytes 6291460
  127.0 3.0 %copy-start.10 = (bf16[256,1024]{1,0:T(8,128)(2,1)S(1)}, bf16[256,1024]{1,0:T(8,128)(2,1)}, u32[]{:S(2)}) copy-start(bf16[256,1024]{1,0:T(8,128)(2,1)} %param.10) | copy-start | bytes 1572868
  132.2 15.9 %copy-start.4 = (bf16[8,256,128]{2,1,0:T(8,128)(2,1)S(1)}, bf16[8,256,128]{2,1,0:T(8,128)(2,1)}, u32[]{:S(2)}) copy-start(bf16[8,256,128]{2,1,0:T(8,128)(2,1)} %get-tuple-element.10) | copy-start | bytes 1572868
  148.1 1.0 copy-start.5
  176.9 31.3 %copy-start.9 = (bf16[1024,256]{0,1:T(8,128)(2,1)S(1)}, bf16[1024,256]{0,1:T(8,128)(2,1)}, u32[]{:S(2)}) copy-start(bf16[1024,256]{0,1:T(8,128)(2,1)} %get-tuple-element.26) | copy-start | bytes 1572868
  206.5 1.7 copy-start.2
  208.2 4.9 %copy-start.1 = (bf16[1024,1024]{1,0:T(8,128)(2,1)S(1)}, bf16[1024,1024]{1,0:T(8,128)(2,1)}, u32[]{:S(2)}) copy-start(bf16[1024,1024]{1,0:T(8,128)(2,1)} %param.9) | copy-start | bytes 6291460

commit v3 on v2

--- a/solution.py
+++ b/solution.py
@@ -202,45 +202,142 @@
     return here + 1 - 2 * lax.rem(here, 2), lax.rem(here + 2, 4)
 
 
-def exchange_kernel(count, x_ref, o_ref, local_sem, send_sem, recv_sem):
+def middle_kernel(
+    count,
+    att_ref,
+    tok_ref,
+    gate_ref,
+    dg_ref,
+    wout_ref,
+    mixed_ref,
+    grad_u_ref,
+    d_heads_ref,
+    att_in,
+    d_out,
+    normed_ref,
+    gated_ref,
+    local_sem,
+    att_sem,
+    d_sem,
+):
     me = lax.axis_index("head")
+    features = att_in.shape[2]
+    local_rows = tok_ref.shape[0]
     others = [lax.rem(me + k, count) for k in range(1, count)]
     greet([{"head": other} for other in others])
-    local = pltpu.make_async_copy(x_ref.at[me], o_ref.at[me], local_sem)
+    local = pltpu.make_async_copy(att_ref.at[me], att_in.at[me], local_sem.at[0])
     local.start()
     copies = [
-        send(x_ref.at[other], o_ref.at[me], send_sem.at[k], recv_sem.at[k], {"head": other})
+        send(att_ref.at[other], att_in.at[me], att_sem.at[0, k], att_sem.at[1, k], {"head": other})
         for k, other in enumerate(others)
     ]
     local.wait()
     for copy in copies:
         copy.wait()
-
-
-def exchange(x, collective_id):
-    count = x.shape[0]
+    step = 64
+    for start in range(0, local_rows, step):
+        rows = slice(start, start + step)
+        attended = jnp.concatenate([att_in[j, rows, :] for j in range(count)], axis=1)
+        attended = attended.astype(jnp.float32)
+        average = jnp.mean(attended, axis=1, keepdims=True)
+        centered = attended - average
+        variance = jnp.mean(centered * centered, axis=1, keepdims=True)
+        inverse_std = lax.rsqrt(variance + epsilon)
+        normed = centered * inverse_std
+        gate = gate_ref[rows, :].astype(jnp.float32)
+        normed_ref[rows, :] = normed
+        gated_ref[rows, :] = (normed * gate).astype(jnp.bfloat16)
+        d_normed = dg_ref[rows, :] * gate
+        d_attended = inverse_std * (
+            d_normed
+            - jnp.mean(d_normed, axis=1, keepdims=True)
+            - normed * jnp.mean(d_normed * normed, axis=1, keepdims=True)
+        )
+        d_attended = d_attended.astype(jnp.bfloat16)
+        for j in range(count):
+            d_out[j, rows, :] = d_attended[:, j * features : (j + 1) * features]
+    local = pltpu.make_async_copy(d_out.at[me], d_heads_ref.at[me], local_sem.at[1])
+    local.start()
+    copies = [
+        send(d_out.at[other], d_heads_ref.at[me], d_sem.at[0, k], d_sem.at[1, k], {"head": other})
+        for k, other in enumerate(others)
+    ]
+    mixed = jnp.dot(gated_ref[...], wout_ref[...], preferred_element_type=jnp.float32)
+    mixed_ref[...] = (tok_ref[...].astype(jnp.float32) + mixed).astype(jnp.bfloat16)
+    grad_u_ref[...] = (dg_ref[...] * normed_ref[...]).T.astype(jnp.bfloat16)
+    local.wait()
+    for copy in copies:
+        copy.wait()
+
+
+def middle(attended, tokens, gate_u, d_gated, w_out):
+    count = attended.shape[0]
+    local_rows, width = tokens.shape
     anywhere = pl.BlockSpec(memory_space=pl.ANY)
+    vmem = pl.BlockSpec(memory_space=pltpu.VMEM)
+    pair = pltpu.SemaphoreType.DMA((2, count - 1))
     return pl.pallas_call(
-        functools.partial(exchange_kernel, count),
-        in_specs=[anywhere],
-        out_specs=anywhere,
-        out_shape=jax.ShapeDtypeStruct(x.shape, x.dtype),
+        functools.partial(middle_kernel, count),
+        in_specs=[anywhere, vmem, vmem, vmem, vmem],
+        out_specs=[vmem, vmem, anywhere],
+        out_shape=[
+            jax.ShapeDtypeStruct(tokens.shape, jnp.bfloat16),
+            jax.ShapeDtypeStruct((width, local_rows), jnp.bfloat16),
+            jax.ShapeDtypeStruct(attended.shape, jnp.bfloat16),
+        ],
         scratch_shapes=[
-            pltpu.SemaphoreType.DMA,
-            pltpu.SemaphoreType.DMA((count - 1,)),
-            pltpu.SemaphoreType.DMA((count - 1,)),
-        ],
-        compiler_params=pltpu.CompilerParams(collective_id=collective_id, has_side_effects=True),
-        name="exchange",
-    )(x)
+            pltpu.VMEM(attended.shape, jnp.bfloat16),
+            pltpu.VMEM(attended.shape, jnp.bfloat16),
+            pltpu.VMEM((local_rows, width), jnp.float32),
+            pltpu.VMEM((local_rows, width), jnp.bfloat16),
+            pltpu.SemaphoreType.DMA((2,)),
+            pair,
+            pair,
+        ],
+        compiler_params=pltpu.CompilerParams(
+            collective_id=1, has_side_effects=True, vmem_limit_bytes=48 * 1024 * 1024
+        ),
+        name="middle",
+    )(attended, tokens, gate_u, d_gated, w_out)
 
 
 def distribute_kernel(
-    count, kv_ref, q_ref, kv_out, q_out, local_sem, kv_sem, q_sem, side_sem, core_sem, pass_sem
+    count,
+    features,
+    tok_ref,
+    w_ref,
+    wout_ref,
+    cot_ref,
+    kv_out,
+    q_out,
+    gate_ref,
+    dg_ref,
+    w_buf,
+    kv_buf,
+    q_buf,
+    w_sem,
+    local_sem,
+    kv_sem,
+    q_sem,
+    side_sem,
+    core_sem,
+    pass_sem,
 ):
     me, here = lax.axis_index("head"), lax.axis_index("blk")
     core, side = blk_partners(here)
-    rows = kv_ref.shape[1]
+    rows, width = tok_ref.shape
+    lanes = 128
+    per = lanes // features
+    groups = count // per
+    own_group, own_member = lax.div(me, per), lax.rem(me, per)
+
+    def fetch(first, last, sem):
+        columns = pl.ds(first * width, (last - first) * width)
+        copy = pltpu.make_async_copy(w_ref.at[:, columns], w_buf.at[:, columns], sem)
+        copy.start()
+        return copy
+
+    fetches = [fetch(2, 4, w_sem.at[0]), fetch(1, 2, w_sem.at[1]), fetch(0, 1, w_sem.at[2])]
     others = [lax.rem(me + k, count) for k in range(1, count)]
     greet([{"head": other} for other in others] + [{"blk": core}, {"blk": side}])
 
@@ -248,69 +345,140 @@
         start = pl.multiple_of((segment * count + source) * rows, rows)
         return kv_out.at[pl.ds(start, rows), :]
 
-    local_kv = pltpu.make_async_copy(kv_ref.at[me], place(here, me), local_sem.at[0])
-    local_kv.start()
-    local_q = pltpu.make_async_copy(q_ref.at[me], q_out.at[me], local_sem.at[1])
-    local_q.start()
-    kv_copies = [
-        send(
-            kv_ref.at[other],
-            place(here, me),
-            kv_sem.at[0, k],
-            kv_sem.at[1, k],
-            {"head": other},
-        )
-        for k, other in enumerate(others)
-    ]
-    q_copies = [
-        send(q_ref.at[other], q_out.at[me], q_sem.at[0, k], q_sem.at[1, k], {"head": other})
-        for k, other in enumerate(others)
-    ]
+    def target(k, j):
+        group = lax.rem(own_group + k, groups)
+        return group * per + lax.rem(own_member + j, per)
+
+    def source(k, j):
+        group = lax.rem(own_group - k + groups, groups)
+        return group * per + lax.rem(own_member - j + per, per)
+
+    def silu_dot(weights):
+        product = jnp.dot(tok_ref[...], weights, preferred_element_type=jnp.float32)
+        half = 0.5 * product
+        return (half + half * jnp.tanh(half)).astype(jnp.bfloat16)
+
+    def columns_of(part, group):
+        start = pl.multiple_of(part * width + group * lanes, lanes)
+        return w_buf[:, pl.ds(start, lanes)]
+
+    kv_copies, q_copies = [], []
+    fetches[0].wait()
+    for k in range(groups):
+        group = lax.rem(own_group + k, groups)
+        both = silu_dot(jnp.concatenate([columns_of(2, group), columns_of(3, group)], axis=1))
+        for j in range(per):
+            keys = both[:, j * features : (j + 1) * features]
+            vals = both[:, lanes + j * features : lanes + (j + 1) * features]
+            kv_buf[group * per + j] = jnp.concatenate([keys, vals], axis=1)
+        for j in range(per):
+            to, index = target(k, j), k * per + j
+            if index == 0:
+                local_kv = pltpu.make_async_copy(
+                    kv_buf.at[me], place(here, me), local_sem.at[0]
+                )
+                local_kv.start()
+                kv_copies.append(local_kv)
+            else:
+                kv_copies.append(
+                    send(
+                        kv_buf.at[to],
+                        place(here, me),
+                        kv_sem.at[0, index],
+                        kv_sem.at[1, index],
+                        {"head": to},
+                    )
+                )
+    fetches[1].wait()
+    for k in range(groups):
+        group = lax.rem(own_group + k, groups)
+        query = silu_dot(columns_of(1, group))
+        for j in range(per):
+            q_buf[group * per + j] = query[:, j * features : (j + 1) * features]
+        for j in range(per):
+            to, index = target(k, j), k * per + j
+            if index == 0:
+                local_q = pltpu.make_async_copy(q_buf.at[me], q_out.at[me], local_sem.at[1])
+                local_q.start()
+            else:
+                q_copies.append(
+                    send(
+                        q_buf.at[to],
+                        q_out.at[me],
+                        q_sem.at[0, index],
+                        q_sem.at[1, index],
+                        {"head": to},
+                    )
+                )
     side_copies, core_copies, pass_copies = [], [], []
     lag = 2
-    for k in range(count + lag):
-        if k < count:
-            if k == 0:
+    for index in range(count + lag):
+        if index < count:
+            if index == 0:
                 local_kv.wait()
             else:
-                kv_copies[k - 1].wait_recv()
-            chunk = place(here, lax.rem(me - k + count, count))
+                kv_copies[index].wait_recv()
+            chunk = place(here, source(index // per, index % per))
             side_copies.append(
-                send(chunk, chunk, side_sem.at[0, k], side_sem.at[1, k], {"blk": side})
+                send(chunk, chunk, side_sem.at[0, index], side_sem.at[1, index], {"blk": side})
             )
             core_copies.append(
-                send(chunk, chunk, core_sem.at[0, k], core_sem.at[1, k], {"blk": core})
+                send(chunk, chunk, core_sem.at[0, index], core_sem.at[1, index], {"blk": core})
             )
-        j = k - lag
+        if index == 1:
+            fetches[2].wait()
+            for c in range(0, width, 256):
+                gate_ref[:, c : c + 256] = silu_dot(w_buf[:, c : c + 256])
+        if index == 2:
+            for c in range(0, width, 256):
+                dg_ref[:, c : c + 256] = dot_nt(cot_ref[...], wout_ref[c : c + 256, :])
+        j = index - lag
         if j >= 0:
             side_copies[j].wait_recv()
-            chunk = place(side, lax.rem(me - j + count, count))
+            chunk = place(side, source(j // per, j % per))
             pass_copies.append(
                 send(chunk, chunk, pass_sem.at[0, j], pass_sem.at[1, j], {"blk": core})
             )
     local_q.wait()
-    for copy in kv_copies + side_copies:
+    for copy in kv_copies[1:] + side_copies:
         copy.wait_send()
     for copy in q_copies + core_copies + pass_copies:
         copy.wait()
 
 
-def distribute(kv, q, groups):
-    count, rows, width = kv.shape
+def distribute(tokens, w_proj, w_out, cotangent, count, groups):
+    rows, width = tokens.shape
+    features = width // count
     anywhere = pl.BlockSpec(memory_space=pl.ANY)
+    vmem = pl.BlockSpec(memory_space=pltpu.VMEM)
     pair = pltpu.SemaphoreType.DMA((2, count))
     return pl.pallas_call(
-        functools.partial(distribute_kernel, count),
-        in_specs=[anywhere, anywhere],
-        out_specs=[anywhere, anywhere],
+        functools.partial(distribute_kernel, count, features),
+        in_specs=[vmem, anywhere, vmem, vmem],
+        out_specs=[anywhere, anywhere, vmem, vmem],
         out_shape=[
-            jax.ShapeDtypeStruct((groups * count * rows, width), kv.dtype),
-            jax.ShapeDtypeStruct(q.shape, q.dtype),
-        ],
-        scratch_shapes=[pltpu.SemaphoreType.DMA((2,)), pair, pair, pair, pair, pair],
-        compiler_params=pltpu.CompilerParams(collective_id=0, has_side_effects=True),
+            jax.ShapeDtypeStruct((groups * count * rows, 2 * features), jnp.bfloat16),
+            jax.ShapeDtypeStruct((count, rows, features), jnp.bfloat16),
+            jax.ShapeDtypeStruct((rows, width), jnp.bfloat16),
+            jax.ShapeDtypeStruct((rows, width), jnp.float32),
+        ],
+        scratch_shapes=[
+            pltpu.VMEM(w_proj.shape, jnp.bfloat16),
+            pltpu.VMEM((count, rows, 2 * features), jnp.bfloat16),
+            pltpu.VMEM((count, rows, features), jnp.bfloat16),
+            pltpu.SemaphoreType.DMA((3,)),
+            pltpu.SemaphoreType.DMA((2,)),
+            pair,
+            pair,
+            pair,
+            pair,
+            pair,
+        ],
+        compiler_params=pltpu.CompilerParams(
+            collective_id=0, has_side_effects=True, vmem_limit_bytes=48 * 1024 * 1024
+        ),
         name="distribute",
-    )(kv, q)
+    )(tokens, w_proj, w_out, cotangent)
 
 
 def collect_kernel(
@@ -383,7 +551,7 @@
             pair,
         ],
         compiler_params=pltpu.CompilerParams(
-            collective_id=3, has_side_effects=True, vmem_limit_bytes=48 * 1024 * 1024
+            collective_id=2, has_side_effects=True, vmem_limit_bytes=48 * 1024 * 1024
         ),
         name="collect",
     )(partial.reshape((groups,) + block), grad_query)
@@ -396,16 +564,8 @@
     local_rows, width = tokens.shape
     features = width // head_count
     segment = local_rows * head_count
-    projected = jax.nn.silu(
-        jnp.dot(tokens, w_proj, preferred_element_type=jnp.float32)
-    ).astype(jnp.bfloat16)
-    gate_u = projected[:, :width].astype(jnp.float32)
-    by_owner = projected[:, width:].reshape(local_rows, 3, head_count, features)
-    key_vals = jnp.concatenate([by_owner[:, 1], by_owner[:, 2]], axis=2)
-    key_all, query = distribute(
-        jnp.transpose(key_vals, (1, 0, 2)),
-        jnp.transpose(by_owner[:, 0], (1, 0, 2)),
-        group_count,
+    key_all, query, gate_u, d_gated = distribute(
+        tokens, w_proj, w_out, cotangent, head_count, group_count
     )
     query = query.reshape(segment, features)
     positions_here = lax.dynamic_slice_in_dim(positions, segment_index * segment, segment, 0)
@@ -413,28 +573,10 @@
     attended, prob, slope = attention_forward(
         key_blocks, weights, query, key_all, positions_here
     )
-    by_token = exchange(attended.reshape(head_count, local_rows, features), 1)
-    by_token = jnp.transpose(by_token, (1, 0, 2)).reshape(local_rows, width)
-    by_token = by_token.astype(jnp.float32)
-    average = jnp.mean(by_token, axis=1, keepdims=True)
-    centered = by_token - average
-    variance = jnp.mean(centered * centered, axis=1, keepdims=True)
-    inverse_std = lax.rsqrt(variance + epsilon)
-    normed = centered * inverse_std
-    gated = (normed * gate_u).astype(jnp.bfloat16)
-    mixed = (
-        tokens.astype(jnp.float32) + jnp.dot(gated, w_out, preferred_element_type=jnp.float32)
-    ).astype(jnp.bfloat16)
-    d_gated = dot_nt(cotangent, w_out)
-    grad_u = (d_gated * normed).astype(jnp.bfloat16).T
-    d_normed = d_gated * gate_u
-    d_attended = inverse_std * (
-        d_normed
-        - jnp.mean(d_normed, axis=1, keepdims=True)
-        - normed * jnp.mean(d_normed * normed, axis=1, keepdims=True)
-    )
-    d_attended = d_attended.astype(jnp.bfloat16).reshape(local_rows, head_count, features)
-    d_heads = exchange(jnp.transpose(d_attended, (1, 0, 2)), 2).reshape(segment, features)
+    mixed, grad_u, d_heads = middle(
+        attended.reshape(head_count, local_rows, features), tokens, gate_u, d_gated, w_out
+    )
+    d_heads = d_heads.reshape(segment, features)
     grad_query, partial = attention_backward(
         key_blocks, query, d_heads, key_all, prob, slope
     )

time: 214 us -> 176 us (0.82)
  local copies, waits for them, and re-layouts: 29.5 us -> 9.85 us
  matrix products: 10 us -> 0 us
  other arithmetic: 7.99 us -> 0.7 us
    dot_general x3 -> x0, matrix products: 10 us -> none  [the longest x1 6.04 us: shards(): jnp.dot(tokens, w_proj, preferred_element_type=jnp.float32)]
    unnamed x28 -> x16, local copies, waits for them, and re-layouts: 17.7 us -> 8.48 us
    slice x3 -> x0, local copies, waits for them, and re-layouts: 6.42 us -> none  [the longest x2 3.88 us: shards(): by_owner = projected[:, width:].reshape(local_rows, 3, head_count, features)]
    convert_element_type x3 -> x0, local copies, waits for them, and re-layouts: 3.08 us -> none  [the longest x2 2.87 us: shards(): by_token = by_token.astype(jnp.float32)]
    reduce_sum x2 -> x0, other arithmetic: 2.51 us -> none  [the longest x1 1.32 us: shards(): variance = jnp.mean(centered * centered, axis=1, keepdims=True)]
    convert_element_type x2 -> x0, other arithmetic: 2.32 us -> none  [the longest x1 1.21 us: shards(): d_attended.astype(jnp.bfloat16).reshape(local_rows, head_count, features)]
    transpose x1 -> x0, other arithmetic: 2.3 us -> none  [shards(): jnp.transpose(key_vals, (1, 0, 2))]
    pallas_call x3 -> x2, Pallas kernels: 78.4 us -> 77.5 us  [the longest x1 45 us: distribute(): pl.pallas_call(functools.partial(distribute_kernel, count, features), in_...]
where the time goes in v3:
time: 176 us; the launch traced here: 175 us
  Pallas kernels  164 us (93%)
  local copies, waits for them, and re-layouts  9.85 us (6%)
    pallas_call x1, Pallas kernels, distribute(): pl.pallas_call(functools.partial(distribute_kernel, count, features), in_...  45 us
    pallas_call x1, Pallas kernels, middle(): pl.pallas_call(functools.partial(middle_kernel, count), in_specs=[anywher...  32.5 us
    pallas_call x1, Pallas kernels, collect(): pl.pallas_call(functools.partial(collect_kernel, chunks), in_specs=[vmem,...  29.2 us
    pallas_call x1, Pallas kernels, attention_forward(): pl.pallas_call(functools.partial(forward_kernel, heads, slots), grid=(loc...  29.1 us
    pallas_call x1, Pallas kernels, attention_backward(): pl.pallas_call(functools.partial(backward_kernel, heads, slots), grid=(lo...  27.8 us
    unnamed x16, local copies, waits for them, and re-layouts  8.48 us

profile of v3, /device:TPU:11, one launch (start us, length us, event | category | flops | bytes accessed | tf_op | source)
XLA Modules:
  0.0 174.8 jit_solution(1423696203146794337)
XLA Ops:
  0.6 0.8 copy.12
  1.4 0.1 reshape.34.kb_ref
  1.5 0.7 convert_log-plus-one_fusion
  2.2 0.1 copy.13
  2.2 0.1 reshape.35.wt_ref
  2.3 0.0 copy-start
  2.4 1.6 copy-done
  3.9 1.0 copy-done.1
  5.0 1.0 copy-done.3
  6.0 45.0 %distribute.1 = (bf16[8192,256]{1,0:T(8,128)(2,1)}, bf16[8,256,128]{2,1,0:T(8,128)(2,1)S(1)}, bf16[256,1024]{1,0:T(8,128)(2,1)S(1)}, f32[256,1024]{1,0:T(8,128)S(1)}) custom-call(bf16[256,1024]{1,0:T(8,128)(2,1)S(1)} %copy-done.1, bf16[1024,4096]{1,0:T(8,128)(2,1)} %w_ref.1, bf16[1024,1024]{1,0:T(8,128)(2,1)S(1)} %copy-done, bf16[256,1024]{1,0:T(8,128)(2,1)S(1)} %copy-done.3), custom_call_target="tpu_custom_call" | custom-call | tf_op jit(solution)/shard_map/distribute/pallas_call | solution.py:455
  51.0 0.0 copy-start.4
  51.0 0.8 copy-done.4
  51.8 0.8 dynamic_slice.3
  52.5 0.4 copy.14.posc_ref
  52.9 0.0 copy-start.5
  52.9 29.1 %attention_forward.1 = (bf16[2048,128]{1,0:T(8,128)(2,1)S(1)}, bf16[16,1024,512]{2,1,0:T(8,128)(2,1)}, bf16[16,1024,512]{2,1,0:T(8,128)(2,1)}) custom-call(s32[128]{0:T(128)S(1)} %reshape.34.kb_ref, f32[128]{0:T(128)S(1)} %reshape.35.wt_ref, bf16[2048,128]{1,0:T(8,128)(2,1)S(1)} %bitcast.8, bf16[8192,256]{1,0:T(8,128)(2,1)} %get-tuple-element.16.kv_ref, ...), custom_call_target="tpu_custom_call" | custom-call | tf_op jit(solution)/shard_map/attention_forward/pallas_call | solution.py:125
  82.0 0.0 copy-done.2
  82.0 0.0 copy-done.5
  82.0 32.5 %middle.1 = (bf16[256,1024]{1,0:T(8,128)(2,1)S(1)}, bf16[1024,256]{1,0:T(8,128)(2,1)S(1)}, bf16[8,256,128]{2,1,0:T(8,128)(2,1)S(1)}) custom-call(bf16[8,256,128]{2,1,0:T(8,128)(2,1)S(1)} %bitcast.11, bf16[256,1024]{1,0:T(8,128)(2,1)S(1)} %copy-done.2, bf16[256,1024]{1,0:T(8,128)(2,1)S(1)} %copy-done.5, f32[256,1024]{1,0:T(8,128)S(1)} %get-tuple-element.19.dg_ref, ...), custom_call_target="tpu_custom_call" | custom-call | tf_op jit(solution)/shard_map/middle/pallas_call | solution.py:279
  114.6 27.8 %attention_backward.1 = (f32[128,2048]{1,0:T(8,128)S(1)}, bf16[8192,256]{1,0:T(8,128)(2,1)}) custom-call(s32[128]{0:T(128)S(1)} %reshape.34.kb_ref, bf16[2048,128]{1,0:T(8,128)(2,1)S(1)} %bitcast.9, bf16[2048,128]{1,0:T(8,128)(2,1)S(1)} %bitcast.10, bf16[8192,256]{1,0:T(8,128)(2,1)} %get-tuple-element.16.kv_ref, ...), custom_call_target="tpu_custom_call" | custom-call | tf_op jit(solution)/shard_map/attention_backward/pallas_call | solution.py:164
  142.3 29.2 %collect.1 = f32[384,2048]{1,0:T(8,128)S(1)} custom-call(bf16[4,8,256,256]{3,2,1,0:T(8,128)(2,1)} %bitcast.14, f32[128,2048]{1,0:T(8,128)S(1)} %get-tuple-element.26.dq_ref), custom_call_target="tpu_custom_call" | custom-call | tf_op jit(solution)/shard_map/collect/pallas_call | solution.py:540
  171.6 0.8 copy.18
  172.4 0.8 copy.19
  173.2 1.7 copy.20
  (3 shorter events, 0.0 us)
Async XLA Ops:
  2.3 1.6 copy-start
  3.9 1.0 copy-start.1
  5.0 1.0 copy-start.3
  51.0 0.8 copy-start.4
  51.8 30.3 %copy-start.2 = (bf16[256,1024]{1,0:T(8,128)(2,1)S(1)}, bf16[256,1024]{1,0:T(8,128)(2,1)}, u32[]{:S(2)}) copy-start(bf16[256,1024]{1,0:T(8,128)(2,1)} %tok_ref.3) | copy-start | bytes 1572868
  52.9 29.1 %copy-start.5 = (bf16[256,1024]{1,0:T(8,128)(2,1)S(1)}, bf16[256,1024]{1,0:T(8,128)(2,1)}, u32[]{:S(2)}) copy-start(bf16[256,1024]{1,0:T(8,128)(2,1)} %copy-done.4) | copy-start | bytes 1572868

commit v4 on v3

--- a/solution.py
+++ b/solution.py
@@ -35,21 +35,15 @@
     )
 
 
-def forward_kernel(
-    heads, slots, kb_ref, wt_ref, q_ref, kv_ref, posc_ref, posr_ref, o_ref, p_ref, g_ref
-):
-    i = pl.program_id(0)
-    width = q_ref.shape[1]
-    q_wide = spread_heads(q_ref[...], heads)
+def forward_block(heads, slots, i, kb_ref, wt_ref, query, kv_ref, posc, posr, p_ref, g_ref):
+    width = query.shape[1]
+    q_wide = spread_heads(query, heads)
     pair = 2
     out_t = None
     for c in range(slots // pair):
-        rows = [
-            pl.ds(pl.multiple_of(kb_ref[i * slots + c * pair + s] * BLOCK, BLOCK), BLOCK)
-            for s in range(pair)
-        ]
-        keys = jnp.concatenate([kv_ref[r, :width] for r in rows], axis=0)
-        vals = jnp.concatenate([kv_ref[r, width:] for r in rows], axis=0)
+        tables = [kv_ref[kb_ref[i * slots + c * pair + s]] for s in range(pair)]
+        keys = jnp.concatenate([table[:, :width] for table in tables], axis=0)
+        vals = jnp.concatenate([table[:, width:] for table in tables], axis=0)
         scores = dot_nt(keys, q_wide)
         probs = []
         for s in range(pair):
@@ -59,19 +53,18 @@
             hu = half * up
             slope = up + hu * (2.0 - up)
             if c == 0 and s == 0:
-                allowed = posc_ref[...] <= posr_ref[0]
-                coefficient = jnp.where(allowed, weight, 0.0)
+                coefficient = jnp.where(posc <= posr, weight, 0.0)
                 coefficient = jnp.concatenate([coefficient] * heads, axis=1)
             else:
                 coefficient = weight
             prob = (hu * coefficient).astype(jnp.bfloat16)
             at = (c * pair + s) * BLOCK
-            p_ref[0, at : at + BLOCK, :] = prob
-            g_ref[0, at : at + BLOCK, :] = (slope * (0.5 * coefficient)).astype(jnp.bfloat16)
+            p_ref[at : at + BLOCK, :] = prob
+            g_ref[at : at + BLOCK, :] = (slope * (0.5 * coefficient)).astype(jnp.bfloat16)
             probs.append(prob)
         part = jnp.dot(vals.T, jnp.concatenate(probs, axis=0), preferred_element_type=jnp.float32)
         out_t = part if out_t is None else out_t + part
-    o_ref[...] = take_heads(out_t, heads).T.astype(jnp.bfloat16)
+    return take_heads(out_t, heads).T.astype(jnp.bfloat16)
 
 
 def backward_kernel(
@@ -114,43 +107,6 @@
         dkv_ref[:, width:] = acc_ref[:, width:].astype(jnp.bfloat16)
 
 
-def attention_forward(key_blocks, weights, query, key_vals, positions_here):
-    local_blocks, slots = key_blocks.shape
-    width = query.shape[1]
-    heads = width // HEAD_DIM
-    wide = heads * BLOCK
-    whole = pl.BlockSpec(memory_space=pltpu.VMEM)
-    smem = pl.BlockSpec(memory_space=pltpu.SMEM)
-    stored = jax.ShapeDtypeStruct((local_blocks, slots * BLOCK, wide), jnp.bfloat16)
-    return pl.pallas_call(
-        functools.partial(forward_kernel, heads, slots),
-        grid=(local_blocks,),
-        in_specs=[
-            smem,
-            smem,
-            pl.BlockSpec((BLOCK, width), lambda i: (i, 0)),
-            whole,
-            pl.BlockSpec((BLOCK, 1), lambda i: (i, 0)),
-            pl.BlockSpec((1, 1, BLOCK), lambda i: (i, 0, 0)),
-        ],
-        out_specs=[
-            pl.BlockSpec((BLOCK, width), lambda i: (i, 0)),
-            pl.BlockSpec((1, slots * BLOCK, wide), lambda i: (i, 0, 0)),
-            pl.BlockSpec((1, slots * BLOCK, wide), lambda i: (i, 0, 0)),
-        ],
-        out_shape=[jax.ShapeDtypeStruct(query.shape, jnp.bfloat16), stored, stored],
-        compiler_params=pltpu.CompilerParams(vmem_limit_bytes=48 * 1024 * 1024),
-        name="attention_forward",
-    )(
-        key_blocks.reshape(-1),
-        weights.reshape(-1),
-        query,
-        key_vals,
-        positions_here.reshape(-1, 1),
-        positions_here.reshape(local_blocks, 1, BLOCK),
-    )
-
-
 def attention_backward(key_blocks, query, d_attended, key_vals, prob, slope):
     local_blocks, slots = key_blocks.shape
     width = query.shape[1]
@@ -204,7 +160,14 @@
 
 def middle_kernel(
     count,
-    att_ref,
+    heads,
+    slots,
+    kb_ref,
+    wt_ref,
+    q_ref,
+    kv_ref,
+    posc_ref,
+    posr_ref,
     tok_ref,
     gate_ref,
     dg_ref,
@@ -212,93 +175,186 @@
     mixed_ref,
     grad_u_ref,
     d_heads_ref,
+    prob_ref,
+    slope_ref,
+    p_buf,
+    g_buf,
+    att_out,
     att_in,
     d_out,
     normed_ref,
     gated_ref,
     local_sem,
+    store_sem,
     att_sem,
     d_sem,
 ):
     me = lax.axis_index("head")
     features = att_in.shape[2]
     local_rows = tok_ref.shape[0]
+    per_owner = local_rows // BLOCK
     others = [lax.rem(me + k, count) for k in range(1, count)]
     greet([{"head": other} for other in others])
-    local = pltpu.make_async_copy(att_ref.at[me], att_in.at[me], local_sem.at[0])
-    local.start()
-    copies = [
-        send(att_ref.at[other], att_in.at[me], att_sem.at[0, k], att_sem.at[1, k], {"head": other})
-        for k, other in enumerate(others)
-    ]
-    local.wait()
-    for copy in copies:
-        copy.wait()
-    step = 64
-    for start in range(0, local_rows, step):
-        rows = slice(start, start + step)
-        attended = jnp.concatenate([att_in[j, rows, :] for j in range(count)], axis=1)
-        attended = attended.astype(jnp.float32)
-        average = jnp.mean(attended, axis=1, keepdims=True)
-        centered = attended - average
-        variance = jnp.mean(centered * centered, axis=1, keepdims=True)
-        inverse_std = lax.rsqrt(variance + epsilon)
-        normed = centered * inverse_std
-        gate = gate_ref[rows, :].astype(jnp.float32)
-        normed_ref[rows, :] = normed
-        gated_ref[rows, :] = (normed * gate).astype(jnp.bfloat16)
-        d_normed = dg_ref[rows, :] * gate
-        d_attended = inverse_std * (
-            d_normed
-            - jnp.mean(d_normed, axis=1, keepdims=True)
-            - normed * jnp.mean(d_normed * normed, axis=1, keepdims=True)
-        )
-        d_attended = d_attended.astype(jnp.bfloat16)
-        for j in range(count):
-            d_out[j, rows, :] = d_attended[:, j * features : (j + 1) * features]
-    local = pltpu.make_async_copy(d_out.at[me], d_heads_ref.at[me], local_sem.at[1])
-    local.start()
-    copies = [
-        send(d_out.at[other], d_heads_ref.at[me], d_sem.at[0, k], d_sem.at[1, k], {"head": other})
-        for k, other in enumerate(others)
-    ]
+
+    def attended_copy(k):
+        owner = lax.rem(me + 1 + k, count)
+        return pltpu.make_async_remote_copy(
+            src_ref=att_out.at[owner],
+            dst_ref=att_in.at[me],
+            send_sem=att_sem.at[0, k],
+            recv_sem=att_sem.at[1, k],
+            device_id={"head": owner},
+            device_id_type=pl.DeviceIdType.MESH,
+        )
+
+    def stores(slot, block):
+        return [
+            pltpu.make_async_copy(p_buf.at[slot], prob_ref.at[block], store_sem.at[0, slot]),
+            pltpu.make_async_copy(g_buf.at[slot], slope_ref.at[block], store_sem.at[1, slot]),
+        ]
+
+    def step(t, carry):
+        k, r = lax.div(t, per_owner), lax.rem(t, per_owner)
+        owner = lax.rem(me + 1 + k, count)
+        block = owner * per_owner + r
+        slot = lax.rem(t, 2)
+
+        @pl.when(t >= 2)
+        def _():
+            for copy in stores(slot, block):
+                copy.wait()
+
+        rows = pl.ds(pl.multiple_of(block * BLOCK, BLOCK), BLOCK)
+        attended = forward_block(
+            heads,
+            slots,
+            block,
+            kb_ref,
+            wt_ref,
+            q_ref[rows, :],
+            kv_ref,
+            posc_ref[rows, :],
+            posr_ref[block],
+            p_buf.at[slot],
+            g_buf.at[slot],
+        )
+        att_out[owner, pl.ds(pl.multiple_of(r * BLOCK, BLOCK), BLOCK), :] = attended
+        for copy in stores(slot, block):
+            copy.start()
+
+        @pl.when((r == per_owner - 1) & (k < count - 1))
+        def _():
+            attended_copy(k).start()
+
+        return carry
+
+    lax.fori_loop(0, count * per_owner, step, 0)
+    att_in[me] = att_out[me]
+    for k in range(count - 1):
+        attended_copy(k).wait()
+    d_copies = []
+    step_rows = 64
+    half_rows = local_rows // 2
+    for part in range(2):
+        for start in range(part * half_rows, (part + 1) * half_rows, step_rows):
+            rows = slice(start, start + step_rows)
+            attended = jnp.concatenate([att_in[j, rows, :] for j in range(count)], axis=1)
+            attended = attended.astype(jnp.float32)
+            average = jnp.mean(attended, axis=1, keepdims=True)
+            centered = attended - average
+            variance = jnp.mean(centered * centered, axis=1, keepdims=True)
+            inverse_std = lax.rsqrt(variance + epsilon)
+            normed = centered * inverse_std
+            gate = gate_ref[rows, :].astype(jnp.float32)
+            normed_ref[rows, :] = normed
+            gated_ref[rows, :] = (normed * gate).astype(jnp.bfloat16)
+            d_normed = dg_ref[rows, :] * gate
+            d_attended = inverse_std * (
+                d_normed
+                - jnp.mean(d_normed, axis=1, keepdims=True)
+                - normed * jnp.mean(d_normed * normed, axis=1, keepdims=True)
+            )
+            d_attended = d_attended.astype(jnp.bfloat16)
+            for j in range(count):
+                d_out[j, rows, :] = d_attended[:, j * features : (j + 1) * features]
+        rows = pl.ds(part * half_rows, half_rows)
+        local = pltpu.make_async_copy(
+            d_out.at[me, rows], d_heads_ref.at[me, rows], local_sem.at[part]
+        )
+        local.start()
+        d_copies.append(local)
+        for k, other in enumerate(others):
+            d_copies.append(
+                send(
+                    d_out.at[other, rows],
+                    d_heads_ref.at[me, rows],
+                    d_sem.at[0, part, k],
+                    d_sem.at[1, part, k],
+                    {"head": other},
+                )
+            )
     mixed = jnp.dot(gated_ref[...], wout_ref[...], preferred_element_type=jnp.float32)
     mixed_ref[...] = (tok_ref[...].astype(jnp.float32) + mixed).astype(jnp.bfloat16)
     grad_u_ref[...] = (dg_ref[...] * normed_ref[...]).T.astype(jnp.bfloat16)
-    local.wait()
-    for copy in copies:
+    for slot in range(2):
+        for copy in stores(slot, me):
+            copy.wait()
+    for copy in d_copies:
         copy.wait()
 
 
-def middle(attended, tokens, gate_u, d_gated, w_out):
-    count = attended.shape[0]
+def middle(key_blocks, weights, query, key_vals, positions_here, tokens, gate_u, d_gated, w_out):
+    local_blocks, slots = key_blocks.shape
     local_rows, width = tokens.shape
+    segment, features = query.shape
+    heads = features // HEAD_DIM
+    count = segment // local_rows
+    exchanged = (count, local_rows, features)
+    tall, wide = slots * BLOCK, heads * BLOCK
     anywhere = pl.BlockSpec(memory_space=pl.ANY)
     vmem = pl.BlockSpec(memory_space=pltpu.VMEM)
-    pair = pltpu.SemaphoreType.DMA((2, count - 1))
+    smem = pl.BlockSpec(memory_space=pltpu.SMEM)
+    stored = jax.ShapeDtypeStruct((local_blocks, tall, wide), jnp.bfloat16)
     return pl.pallas_call(
-        functools.partial(middle_kernel, count),
-        in_specs=[anywhere, vmem, vmem, vmem, vmem],
-        out_specs=[vmem, vmem, anywhere],
+        functools.partial(middle_kernel, count, heads, slots),
+        in_specs=[smem, smem] + [vmem] * 8,
+        out_specs=[vmem, vmem, anywhere, anywhere, anywhere],
         out_shape=[
             jax.ShapeDtypeStruct(tokens.shape, jnp.bfloat16),
             jax.ShapeDtypeStruct((width, local_rows), jnp.bfloat16),
-            jax.ShapeDtypeStruct(attended.shape, jnp.bfloat16),
+            jax.ShapeDtypeStruct(exchanged, jnp.bfloat16),
+            stored,
+            stored,
         ],
         scratch_shapes=[
-            pltpu.VMEM(attended.shape, jnp.bfloat16),
-            pltpu.VMEM(attended.shape, jnp.bfloat16),
+            pltpu.VMEM((2, tall, wide), jnp.bfloat16),
+            pltpu.VMEM((2, tall, wide), jnp.bfloat16),
+            pltpu.VMEM(exchanged, jnp.bfloat16),
+            pltpu.VMEM(exchanged, jnp.bfloat16),
+            pltpu.VMEM(exchanged, jnp.bfloat16),
             pltpu.VMEM((local_rows, width), jnp.float32),
             pltpu.VMEM((local_rows, width), jnp.bfloat16),
             pltpu.SemaphoreType.DMA((2,)),
-            pair,
-            pair,
+            pltpu.SemaphoreType.DMA((2, 2)),
+            pltpu.SemaphoreType.DMA((2, count - 1)),
+            pltpu.SemaphoreType.DMA((2, 2, count - 1)),
         ],
         compiler_params=pltpu.CompilerParams(
             collective_id=1, has_side_effects=True, vmem_limit_bytes=48 * 1024 * 1024
         ),
         name="middle",
-    )(attended, tokens, gate_u, d_gated, w_out)
+    )(
+        key_blocks.reshape(-1),
+        weights.reshape(-1),
+        query,
+        key_vals.reshape(-1, BLOCK, 2 * features),
+        positions_here.reshape(-1, 1),
+        positions_here.reshape(local_blocks, 1, BLOCK),
+        tokens,
+        gate_u,
+        d_gated,
+        w_out,
+    )
 
 
 def distribute_kernel(
@@ -313,6 +369,8 @@
     gate_ref,
     dg_ref,
     w_buf,
+    wout_buf,
+    cot_buf,
     kv_buf,
     q_buf,
     w_sem,
@@ -338,6 +396,12 @@
         return copy
 
     fetches = [fetch(2, 4, w_sem.at[0]), fetch(1, 2, w_sem.at[1]), fetch(0, 1, w_sem.at[2])]
+    late = [
+        pltpu.make_async_copy(wout_ref, wout_buf, w_sem.at[3]),
+        pltpu.make_async_copy(cot_ref, cot_buf, w_sem.at[4]),
+    ]
+    for copy in late:
+        copy.start()
     others = [lax.rem(me + k, count) for k in range(1, count)]
     greet([{"head": other} for other in others] + [{"blk": core}, {"blk": side}])
 
@@ -430,8 +494,10 @@
             for c in range(0, width, 256):
                 gate_ref[:, c : c + 256] = silu_dot(w_buf[:, c : c + 256])
         if index == 2:
+            for copy in late:
+                copy.wait()
             for c in range(0, width, 256):
-                dg_ref[:, c : c + 256] = dot_nt(cot_ref[...], wout_ref[c : c + 256, :])
+                dg_ref[:, c : c + 256] = dot_nt(cot_buf[...], wout_buf[c : c + 256, :])
         j = index - lag
         if j >= 0:
             side_copies[j].wait_recv()
@@ -454,7 +520,7 @@
     pair = pltpu.SemaphoreType.DMA((2, count))
     return pl.pallas_call(
         functools.partial(distribute_kernel, count, features),
-        in_specs=[vmem, anywhere, vmem, vmem],
+        in_specs=[vmem, anywhere, anywhere, anywhere],
         out_specs=[anywhere, anywhere, vmem, vmem],
         out_shape=[
             jax.ShapeDtypeStruct((groups * count * rows, 2 * features), jnp.bfloat16),
@@ -464,9 +530,11 @@
         ],
         scratch_shapes=[
             pltpu.VMEM(w_proj.shape, jnp.bfloat16),
+            pltpu.VMEM(w_out.shape, jnp.bfloat16),
+            pltpu.VMEM(cotangent.shape, jnp.bfloat16),
             pltpu.VMEM((count, rows, 2 * features), jnp.bfloat16),
             pltpu.VMEM((count, rows, features), jnp.bfloat16),
-            pltpu.SemaphoreType.DMA((3,)),
+            pltpu.SemaphoreType.DMA((5,)),
             pltpu.SemaphoreType.DMA((2,)),
             pair,
             pair,
@@ -570,11 +638,8 @@
     query = query.reshape(segment, features)
     positions_here = lax.dynamic_slice_in_dim(positions, segment_index * segment, segment, 0)
     weights = jnp.log1p(exposures.astype(jnp.float32))
-    attended, prob, slope = attention_forward(
-        key_blocks, weights, query, key_all, positions_here
-    )
-    mixed, grad_u, d_heads = middle(
-        attended.reshape(head_count, local_rows, features), tokens, gate_u, d_gated, w_out
+    mixed, grad_u, d_heads, prob, slope = middle(
+        key_blocks, weights, query, key_all, positions_here, tokens, gate_u, d_gated, w_out
     )
     d_heads = d_heads.reshape(segment, features)
     grad_query, partial = attention_backward(

time: 176 us -> 161 us (0.915)
  Pallas kernels: 164 us -> 150 us
    pallas_call x2 -> x1, Pallas kernels: 61.6 us -> 48.1 us  [middle(): pl.pallas_call(functools.partial(middle_kernel, count, heads, slots), in_...]
    unnamed x16 -> x10, local copies, waits for them, and re-layouts: 8.48 us -> 7.68 us
where the time goes in v4:
time: 161 us
  Pallas kernels  150 us (93%)
  local copies, waits for them, and re-layouts  9 us (6%)
    pallas_call x1, Pallas kernels, middle(): pl.pallas_call(functools.partial(middle_kernel, count, heads, slots), in_...  48.1 us
    pallas_call x1, Pallas kernels, distribute(): pl.pallas_call(functools.partial(distribute_kernel, count, features), in_...  45 us
    pallas_call x1, Pallas kernels, collect(): pl.pallas_call(functools.partial(collect_kernel, chunks), in_specs=[vmem,...  29.4 us
    pallas_call x1, Pallas kernels, attention_backward(): pl.pallas_call(functools.partial(backward_kernel, heads, slots), grid=(lo...  27.8 us
    unnamed x10, local copies, waits for them, and re-layouts  7.68 us

profile of v4, /device:TPU:11, one launch (start us, length us, event | category | flops | bytes accessed | tf_op | source)
XLA Modules:
  0.0 160.7 jit_solution(2094078274371855603)
XLA Ops:
  0.6 0.7 convert_log-plus-one_fusion
  1.3 0.1 copy.13
  1.4 0.1 reshape.35.wt_ref
  1.5 0.7 dynamic_slice.3
  2.2 0.8 copy.12
  3.0 0.1 reshape.34.kb_ref
  3.0 0.4 copy.14.posc_ref
  3.4 0.0 copy-start
  3.4 1.6 copy-done
  5.0 0.0 copy-start.1
  5.0 1.0 copy-done.1
  6.1 0.0 copy-start.2
  6.1 1.0 copy-done.2
  7.1 45.0 %distribute.1 = (bf16[8192,256]{1,0:T(8,128)(2,1)}, bf16[8,256,128]{2,1,0:T(8,128)(2,1)S(1)}, bf16[256,1024]{1,0:T(8,128)(2,1)S(1)}, f32[256,1024]{1,0:T(8,128)S(1)}) custom-call(bf16[256,1024]{1,0:T(8,128)(2,1)S(1)} %copy-done.1, bf16[1024,4096]{1,0:T(8,128)(2,1)} %w_ref.1, bf16[1024,1024]{1,0:T(8,128)(2,1)S(1)} %copy-done, bf16[256,1024]{1,0:T(8,128)(2,1)S(1)} %copy-done.2), custom_call_target="tpu_custom_call" | custom-call | tf_op jit(solution)/shard_map/distribute/pallas_call | solution.py:521
  52.1 48.1 %middle.1 = (bf16[256,1024]{1,0:T(8,128)(2,1)S(1)}, bf16[1024,256]{1,0:T(8,128)(2,1)S(1)}, bf16[8,256,128]{2,1,0:T(8,128)(2,1)S(1)}, bf16[16,1024,512]{2,1,0:T(8,128)(2,1)}, bf16[16,1024,512]{2,1,0:T(8,128)(2,1)}) custom-call(s32[128]{0:T(128)S(1)} %reshape.34.kb_ref, f32[128]{0:T(128)S(1)} %reshape.35.wt_ref, bf16[2048,128]{1,0:T(8,128)(2,1)S(1)} %bitcast.8, ...), custom_call_target="tpu_custom_call" | custom-call | tf_op jit(solution)/shard_map/middle/pallas_call | solution.py:318
  100.2 27.8 %attention_backward.1 = (f32[128,2048]{1,0:T(8,128)S(1)}, bf16[8192,256]{1,0:T(8,128)(2,1)}) custom-call(s32[128]{0:T(128)S(1)} %reshape.34.kb_ref, bf16[2048,128]{1,0:T(8,128)(2,1)S(1)} %bitcast.9, bf16[2048,128]{1,0:T(8,128)(2,1)S(1)} %bitcast.10, bf16[8192,256]{1,0:T(8,128)(2,1)} %get-tuple-element.15.kv_ref, ...), custom_call_target="tpu_custom_call" | custom-call | tf_op jit(solution)/shard_map/attention_backward/pallas_call | solution.py:120
  128.0 29.4 %collect.1 = f32[384,2048]{1,0:T(8,128)S(1)} custom-call(bf16[4,8,256,256]{3,2,1,0:T(8,128)(2,1)} %bitcast.14, f32[128,2048]{1,0:T(8,128)S(1)} %get-tuple-element.24.dq_ref), custom_call_target="tpu_custom_call" | custom-call | tf_op jit(solution)/shard_map/collect/pallas_call | solution.py:608
  157.4 0.8 copy.18
  158.2 0.8 copy.19
  159.0 1.7 %copy.20 = f32[3,128,2048]{2,1,0:T(8,128)} copy(f32[3,128,2048]{2,1,0:T(8,128)S(1)} %bitcast.7) | data formatting | bytes 6291456
Async XLA Ops:
  3.4 1.6 copy-start
  5.0 1.0 copy-start.1
  6.1 1.0 copy-start.2

commit v5 on v4

--- a/solution.py
+++ b/solution.py
@@ -40,11 +40,18 @@
     q_wide = spread_heads(query, heads)
     pair = 2
     out_t = None
-    for c in range(slots // pair):
+
+    def pair_scores(c):
         tables = [kv_ref[kb_ref[i * slots + c * pair + s]] for s in range(pair)]
         keys = jnp.concatenate([table[:, :width] for table in tables], axis=0)
         vals = jnp.concatenate([table[:, width:] for table in tables], axis=0)
-        scores = dot_nt(keys, q_wide)
+        return dot_nt(keys, q_wide), vals
+
+    ahead = pair_scores(0)
+    for c in range(slots // pair):
+        scores, vals = ahead
+        if c + 1 < slots // pair:
+            ahead = pair_scores(c + 1)
         probs = []
         for s in range(pair):
             weight = wt_ref[i * slots + c * pair + s]
@@ -81,17 +88,25 @@
     do_wide = spread_heads(do_ref[...], heads)
     pair = 2
     dq_t = None
-    for c in range(slots // pair):
+
+    def pair_d_probs(c):
         rows = [
             pl.ds(pl.multiple_of(kb_ref[i * slots + c * pair + s] * BLOCK, BLOCK), BLOCK)
             for s in range(pair)
         ]
         keys = jnp.concatenate([kv_ref[r, :width] for r in rows], axis=0)
         vals = jnp.concatenate([kv_ref[r, width:] for r in rows], axis=0)
+        return rows, keys, dot_nt(vals, do_wide)
+
+    ahead = pair_d_probs(0)
+    for c in range(slots // pair):
+        rows, keys, d_probs = ahead
+        if c + 1 < slots // pair:
+            ahead = pair_d_probs(c + 1)
         at = c * pair * BLOCK
         prob = p_ref[0, at : at + pair * BLOCK, :]
         slope = g_ref[0, at : at + pair * BLOCK, :]
-        d_scores = (dot_nt(vals, do_wide) * slope.astype(jnp.float32)).astype(jnp.bfloat16)
+        d_scores = (d_probs * slope.astype(jnp.float32)).astype(jnp.bfloat16)
         d_vals = jnp.dot(prob, do_wide, preferred_element_type=jnp.float32)
         d_keys = jnp.dot(d_scores, q_wide, preferred_element_type=jnp.float32)
         part = jnp.dot(keys.T, d_scores, preferred_element_type=jnp.float32)

time: 161 us -> 157 us (0.975)
  Pallas kernels: 150 us -> 146 us
    pallas_call x1, Pallas kernels: 48.1 us -> 43.6 us  [middle(): pl.pallas_call(functools.partial(middle_kernel, count, heads, slots), in_...]
where the time goes in v5:
time: 157 us; the launch traced here: 156 us
  Pallas kernels  146 us (93%)
  local copies, waits for them, and re-layouts  9 us (6%)
    pallas_call x1, Pallas kernels, distribute(): pl.pallas_call(functools.partial(distribute_kernel, count, features), in_...  45 us
    pallas_call x1, Pallas kernels, middle(): pl.pallas_call(functools.partial(middle_kernel, count, heads, slots), in_...  43.6 us
    pallas_call x1, Pallas kernels, collect(): pl.pallas_call(functools.partial(collect_kernel, chunks), in_specs=[vmem,...  29.5 us
    pallas_call x1, Pallas kernels, attention_backward(): pl.pallas_call(functools.partial(backward_kernel, heads, slots), grid=(lo...  27.8 us
    unnamed x10, local copies, waits for them, and re-layouts  7.68 us

profile of v5, /device:TPU:11, one launch (start us, length us, event | category | flops | bytes accessed | tf_op | source)
XLA Modules:
  0.0 156.2 jit_solution(12432808330324257005)
XLA Ops:
  0.6 0.7 convert_log-plus-one_fusion
  1.3 0.1 copy.13
  1.4 0.1 reshape.35.wt_ref
  1.5 0.7 dynamic_slice.3
  2.2 0.8 copy.12
  3.0 0.1 reshape.34.kb_ref
  3.0 0.4 copy.14.posc_ref
  3.4 0.0 copy-start
  3.4 1.6 %copy-done = bf16[1024,1024]{1,0:T(8,128)(2,1)S(1)} copy-done((bf16[1024,1024]{1,0:T(8,128)(2,1)S(1)}, bf16[1024,1024]{1,0:T(8,128)(2,1)}, u32[]{:S(2)}) %copy-start) | copy-done | bytes 2097176
  5.0 0.0 copy-start.1
  5.0 1.0 copy-done.1
  6.1 0.0 copy-start.2
  6.1 1.0 copy-done.2
  7.1 45.0 %distribute.1 = (bf16[8192,256]{1,0:T(8,128)(2,1)}, bf16[8,256,128]{2,1,0:T(8,128)(2,1)S(1)}, bf16[256,1024]{1,0:T(8,128)(2,1)S(1)}, f32[256,1024]{1,0:T(8,128)S(1)}) custom-call(bf16[256,1024]{1,0:T(8,128)(2,1)S(1)} %copy-done.1, bf16[1024,4096]{1,0:T(8,128)(2,1)} %w_ref.1, bf16[1024,1024]{1,0:T(8,128)(2,1)S(1)} %copy-done, bf16[256,1024]{1,0:T(8,128)(2,1)S(1)} %copy-done.2), custom_call_target="tpu_custom_call" | custom-call | tf_op jit(solution)/shard_map/distribute/pallas_call | solution.py:536
  52.1 43.6 %middle.1 = (bf16[256,1024]{1,0:T(8,128)(2,1)S(1)}, bf16[1024,256]{1,0:T(8,128)(2,1)S(1)}, bf16[8,256,128]{2,1,0:T(8,128)(2,1)S(1)}, bf16[16,1024,512]{2,1,0:T(8,128)(2,1)}, bf16[16,1024,512]{2,1,0:T(8,128)(2,1)}) custom-call(s32[128]{0:T(128)S(1)} %reshape.34.kb_ref, f32[128]{0:T(128)S(1)} %reshape.35.wt_ref, bf16[2048,128]{1,0:T(8,128)(2,1)S(1)} %bitcast.8, ...), custom_call_target="tpu_custom_call" | custom-call | tf_op jit(solution)/shard_map/middle/pallas_call | solution.py:333
  95.7 27.8 %attention_backward.1 = (f32[128,2048]{1,0:T(8,128)S(1)}, bf16[8192,256]{1,0:T(8,128)(2,1)}) custom-call(s32[128]{0:T(128)S(1)} %reshape.34.kb_ref, bf16[2048,128]{1,0:T(8,128)(2,1)S(1)} %bitcast.9, bf16[2048,128]{1,0:T(8,128)(2,1)S(1)} %bitcast.10, bf16[8192,256]{1,0:T(8,128)(2,1)} %get-tuple-element.15.kv_ref, ...), custom_call_target="tpu_custom_call" | custom-call | tf_op jit(solution)/shard_map/attention_backward/pallas_call | solution.py:135
  123.4 29.5 %collect.1 = f32[384,2048]{1,0:T(8,128)S(1)} custom-call(bf16[4,8,256,256]{3,2,1,0:T(8,128)(2,1)} %bitcast.14, f32[128,2048]{1,0:T(8,128)S(1)} %get-tuple-element.24.dq_ref), custom_call_target="tpu_custom_call" | custom-call | tf_op jit(solution)/shard_map/collect/pallas_call | solution.py:623
  152.9 0.8 copy.18
  153.7 0.8 copy.19
  154.5 1.7 %copy.20 = f32[3,128,2048]{2,1,0:T(8,128)} copy(f32[3,128,2048]{2,1,0:T(8,128)S(1)} %bitcast.7) | data formatting | bytes 6291456
Async XLA Ops:
  3.4 1.6 %copy-start = (bf16[1024,1024]{1,0:T(8,128)(2,1)S(1)}, bf16[1024,1024]{1,0:T(8,128)(2,1)}, u32[]{:S(2)}) copy-start(bf16[1024,1024]{1,0:T(8,128)(2,1)} %wout_ref.3) | copy-start | bytes 6291460
  5.0 1.0 copy-start.1
  6.1 1.0 copy-start.2
